TPU v7x, 128 devices: a whole 4x4x4 slice. The times are simulated.
128 devices in a mesh: tm: 8 (over z_lo, x), chan: 16 (over z_hi, y, core).
Axes of the slice: x: 4, y: 4, z: 4 (z_hi: 2, z_lo: 2; z = z_hi * 2 + z_lo), core: 2. Of those that a mesh axis runs over, the one named last changes fastest.
Arguments:
- record: bfloat16 [65536, 2048], P('tm', 'chan'), may hold values from -6 to 6
- starts: int32 [16], P('tm'), may hold values from 0 to 5192
Outputs:
- correlation: float32 [200, 2048, 128], P('tm', 'chan')
Inputs may be any that keep to these rules, and one draw needn't show every extreme that they name: `starts`: each window lies inside its own group's 8192 samples.
All inputs are finite; a program needn't handle non-finite values.
Results may differ from a plain program's by a relative error of at most 0.0071.
Values may be sent and summed in bfloat16 or wider, within the bound.
A program may use at most 256 MiB of HBM per device.

v0:
```python
import math

import jax
import jax.numpy as jnp
from jax import lax
from jax.sharding import PartitionSpec as P

SAMP = 3000
F = 1501
BAND = 200
LAGS = 128


def from_behind(block, axis, distance):
    devices = range(lax.axis_size(axis))
    route = [(i - distance, i) for i in devices if i - distance in devices]
    return lax.ppermute(block, axis, route)


def dft_rows(rows):
    freq = jnp.arange(rows, dtype=jnp.int32)
    times = jnp.arange(SAMP, dtype=jnp.int32)
    phase = freq[:, None] * times[None, :] % SAMP
    angle = phase.astype(jnp.float32) * jnp.float32(2.0 * math.pi / SAMP)
    factor = (freq < F).astype(jnp.float32)[:, None] * jnp.float32(1.0 / math.sqrt(SAMP))
    return jnp.concatenate([jnp.cos(angle) * factor, -jnp.sin(angle) * factor], axis=0).astype(
        jnp.bfloat16
    )


def lag_rows(rows, windows):
    freq = jnp.arange(rows, dtype=jnp.int32)
    moved = jnp.arange(LAGS, dtype=jnp.int32) - LAGS // 2 + SAMP
    phase = freq[:, None] * moved[None, :] % SAMP
    angle = phase.astype(jnp.float32) * jnp.float32(2.0 * math.pi / SAMP)
    weight = jnp.where((freq == 0) | (freq == SAMP // 2), jnp.float32(1.0), jnp.float32(2.0))
    weight = weight * (freq < F).astype(jnp.float32)
    factor = weight[:, None] * jnp.float32(1.0 / math.sqrt(SAMP * windows))
    return jnp.stack([jnp.cos(angle) * factor, -jnp.sin(angle) * factor]).astype(jnp.bfloat16)


def whiten(spec):
    parts = spec.reshape(2, spec.shape[0] // 2, spec.shape[1])
    power = parts[0] * parts[0] + parts[1] * parts[1]
    padded = jnp.pad(power, ((1, 1), (0, 0)))
    smooth = (padded[:-2] + power + padded[2:]) / 3.0
    factor = 1.0 / jnp.maximum(jnp.sqrt(smooth), 0.5)
    return (parts * factor[None]).astype(jnp.bfloat16)


def conj_sum(own, partner):
    real_own = own[..., 0, :, :].astype(jnp.float32)
    imag_own = own[..., 1, :, :].astype(jnp.float32)
    real_far = partner[..., 0, :, :].astype(jnp.float32)
    imag_far = partner[..., 1, :, :].astype(jnp.float32)
    real = jnp.sum(real_own * real_far + imag_own * imag_far, axis=-3)
    imag = jnp.sum(imag_own * real_far - real_own * imag_far, axis=-3)
    return jnp.stack([real, imag], axis=-3).astype(jnp.bfloat16)


def extend(spectra):
    width = spectra.shape[3]
    hops = -(-BAND // width)
    pieces = [spectra]
    for step in range(1, hops + 1):
        pieces.append(from_behind(spectra, "chan", -step))
    return jnp.concatenate(pieces, axis=3)[..., : width + BAND]


def offset_block(own, extended, lags, base, count):
    width = own.shape[3]
    partners = jax.vmap(lambda offset: lax.dynamic_slice_in_dim(extended, offset, width, 3))(
        base + jnp.arange(count, dtype=jnp.int32)
    )
    cross = conj_sum(own, partners)
    return jnp.einsum("ksfc,sft->kct", cross, lags, preferred_element_type=jnp.float32)


def own_offsets(every, extended, lags, rows, width):
    block = math.gcd(rows, 5)
    first = lax.axis_index("tm") * rows + 1

    def per_block(index):
        return offset_block(every, extended, lags, first + index * block, block)

    result = lax.map(per_block, jnp.arange(rows // block, dtype=jnp.int32))
    return result.reshape(rows, width, LAGS)


def body(record, starts):
    groups = lax.axis_size("tm")
    width = record.shape[1]
    padded_bins = -(-F // groups) * groups
    table = dft_rows(padded_bins)

    def one_window(first):
        samples = lax.dynamic_slice_in_dim(record, first, SAMP, 0)
        return whiten(jnp.dot(table, samples, preferred_element_type=jnp.float32))

    white = lax.map(one_window, starts)
    windows = white.shape[0] * groups
    lags = lag_rows(padded_bins, windows)
    rows = BAND // groups
    every = lax.all_gather(white, "tm", axis=0, tiled=True)
    extended = extend(every)
    correlation = own_offsets(every, extended, lags, rows, width)
    return correlation


def solution(mesh):
    return jax.shard_map(
        body,
        mesh=mesh,
        in_specs=(P("tm", "chan"), P("tm")),
        out_specs=P("tm", "chan", None),
        check_vma=False,
    )
```

profile of v0, /device:TPU:24, one launch (start us, length us, event | category | flops | bytes accessed | tf_op | source)
XLA Modules:
  0.0 1318.3 jit_solution(1534050472671562387)
XLA Ops:
  6.5 78.8 %multiply_convert_fusion.2 = (bf16[1504,3000]{1,0:T(8,128)(2,1)}, bf16[1504,3000]{1,0:T(8,128)(2,1)}) fusion(f32[1504]{0:T(1024)S(1)} %fusion.32), kind=kLoop, calls=%fused_computation.42 | loop fusion | flops 63168000 | bytes 18054016 | tf_op jit(solution)/shard_map/convert.10
  85.3 15.7 %pad_maximum_fusion.2 = bf16[3008,3000]{1,0:T(8,128)(2,1)} fusion(bf16[1504,3000]{1,0:T(8,128)(2,1)} %get-tuple-element.156, bf16[1504,3000]{1,0:T(8,128)(2,1)} %get-tuple-element.155), kind=kLoop, calls=%fused_computation.40 | loop fusion | flops 36096000 | bytes 36096000 | tf_op jit(solution)/shard_map/concatenate | solution.py:26
  101.1 24.3 %while.24 = (s32[]{:T(128)}, bf16[2,2,1504,128]{3,2,0,1:T(8,128)(2,1)S(1)}, s32[2]{0:T(128)S(1)}, bf16[8192,128]{1,0:T(8,128)(2,1)}, bf16[3008,3000]{1,0:T(8,128)(2,1)}, /*index=5*/s32[]{:T(128)}, s32[]{:T(128)}, s32[]{:T(128)}) while((s32[]{:T(128)}, bf16[2,2,1504,128]{3,2,0,1:T(8,128)(2,1)S(1)}, s32[2]{0:T(128)S(1)}, ...), condition=%wide.region_1.2_spmd, body=%wide.region_0.1_spmd.sunk | while | flops 2312454144 | bytes 27719820 | solution.py:100
  126.6 131.1 %all-gather.2.cloned.1.call-done = bf16[16,2,1504,128]{3,2,0,1:T(8,128)(2,1)} async-done(((bf16[2,2,1504,128]{3,2,0,1:T(8,128)(2,1)}), bf16[16,2,1504,128]{3,2,0,1:T(8,128)(2,1)}) %all-gather.2.cloned.1.call-update) | async-done | bytes 12320784 | tf_op jit(solution)/shard_map/all_gather | solution.py:104
  276.5 257.0 %collective-permute-done = bf16[16,2,1504,128]{3,2,1,0:T(8,128)(2,1)} collective-permute-done((bf16[16,2,1504,128]{3,2,1,0:T(8,128)(2,1)}, bf16[16,2,1504,128]{3,2,1,0:T(8,128)(2,1)}, u32[]{:S(2)}, u32[]{:S(2)}) %collective-permute-start) | collective-permute-done | bytes 12320800 | tf_op jit(solution)/shard_map/ppermute | solution.py:17
  533.5 139.4 %collective-permute-done.1 = bf16[16,2,1504,128]{3,2,1,0:T(8,128)(2,1)} collective-permute-done((bf16[16,2,1504,128]{3,2,1,0:T(8,128)(2,1)}, bf16[16,2,1504,128]{3,2,1,0:T(8,128)(2,1)}, u32[]{:S(2)}, u32[]{:S(2)}) %collective-permute-start.1) | collective-permute-done | bytes 12320800 | tf_op jit(solution)/shard_map/ppermute | solution.py:17
  672.8 25.2 %pad_maximum_fusion = bf16[16,2,1504,328]{3,2,1,0:T(8,128)(2,1)} fusion(bf16[16,2,1504,128]{3,2,1,0:T(8,128)(2,1)} %collective-permute-done.1, bf16[16,2,1504,128]{3,2,1,0:T(8,128)(2,1)} %collective-permute-done, bf16[16,2,1504,128]{3,2,0,1:T(8,128)(2,1)} %all-gather.2.cloned.1.call-done), kind=kLoop, calls=%fused_computation.35 | loop fusion | flops 94715904 | bytes 68534272 | tf_op jit(solution)/shard_map/concatenate | solution.py:67
  698.0 613.4 %while.26 = (s32[]{:T(128)}, f32[5,5,128,128]{3,2,1,0:T(8,128)}, bf16[16,2,1504,128]{3,2,0,1:T(8,128)(2,1)}, s32[5]{0:T(128)S(1)}, s32[]{:T(128)}, /*index=5*/bf...) while((s32[]{:T(128)}, f32[5,5,128,128]{3,2,1,0:T(8,128)}, ...), condition=%wide.region_5.6_spmd, body=%wide.region_2.5_spmd.sunk | while | flops 653000768 | bytes 156649488 | solution.py:86
  699.4 77.7 %while.27 = (s32[]{:T(128)}, bf16[16,2,1504,328]{3,2,1,0:T(8,128)(2,1)}, s32[5,4]{0,1:T(4,128)S(1)}, bf16[5,16,2,1504,128]{4,3,2,1,0:T(8,128)(2,1)}, s32[]{:T(128)}) while((s32[]{:T(128)}, bf16[16,2,1504,328]{3,2,1,0:T(8,128)(2,1)}, s32[5,4]{0,1:T(4,128)S(1)}, bf16[5,16,2,1504,128]{4,3,2,1,0:T(8,128)(2,1)}, s32[]{:T(128)}) %tuple.62), condition=%wide.while_cond, body=%wide.while_body.sunk | while | flops 2 | bytes 24642664 | solution.py:72
  700.1 14.9 %bitcast_dynamic-update-slice_fusion.2 = bf16[5,16,2,1504,128]{4,3,2,1,0:T(8,128)(2,1)} fusion(bf16[5,16,2,1504,128]{4,3,2,1,0:T(8,128)(2,1)} %get-tuple-element.283, s32[]{:T(128)} %get-tuple-element.280, bf16[16,2,1504,328]{3,2,1,0:T(8,128)(2,1)} %get-tuple-element.286, s32[]{:T(128)} %bitcast.75), kind=kLoop, calls=%fused_computation.10.clone.1 | loop fusion | bytes 24642560 | tf_op jit(solution)/shard_map/while/body/eval_jaxpr/vmap()/gather
  762.2 14.9 %bitcast_dynamic-update-slice_fusion.2 = bf16[5,16,2,1504,128]{4,3,2,1,0:T(8,128)(2,1)} fusion(bf16[5,16,2,1504,128]{4,3,2,1,0:T(8,128)(2,1)} %get-tuple-element.283, s32[]{:T(128)} %get-tuple-element.280, bf16[16,2,1504,328]{3,2,1,0:T(8,128)(2,1)} %get-tuple-element.286, s32[]{:T(128)} %bitcast.75), kind=kLoop, calls=%fused_computation.10.clone.1 | loop fusion | bytes 24642560 | tf_op jit(solution)/shard_map/while/body/eval_jaxpr/vmap()/gather
  783.5 33.2 %fusion.55 = (bf16[5,1504,128]{2,1,0:T(8,128)(2,1)}, bf16[5,1504,128]{2,1,0:T(8,128)(2,1)}) fusion(f32[16,1504,128]{2,1,0:T(8,128)S(1)} %get-tuple-element.265, f32[16,1504,128]{2,1,0:T(8,128)S(1)} %get-tuple-element.266, bf16[5,16,2,1504,128]{4,3,2,1,0:T(8,128)(2,1)} %get-tuple-element.267), kind=kLoop, calls=%fused_computation.17.clone.1 | loop fusion | flops 152084480 | bytes 90095616 | tf_op jit(solution)/shard_map/while/body/eval_jaxpr/reduce_sum | solution.py:56
  822.1 77.7 %while.27 = (s32[]{:T(128)}, bf16[16,2,1504,328]{3,2,1,0:T(8,128)(2,1)}, s32[5,4]{0,1:T(4,128)S(1)}, bf16[5,16,2,1504,128]{4,3,2,1,0:T(8,128)(2,1)}, s32[]{:T(128)}) while((s32[]{:T(128)}, bf16[16,2,1504,328]{3,2,1,0:T(8,128)(2,1)}, s32[5,4]{0,1:T(4,128)S(1)}, bf16[5,16,2,1504,128]{4,3,2,1,0:T(8,128)(2,1)}, s32[]{:T(128)}) %tuple.62), condition=%wide.while_cond, body=%wide.while_body.sunk | while | flops 2 | bytes 24642664 | solution.py:72
  822.8 14.9 %bitcast_dynamic-update-slice_fusion.2 = bf16[5,16,2,1504,128]{4,3,2,1,0:T(8,128)(2,1)} fusion(bf16[5,16,2,1504,128]{4,3,2,1,0:T(8,128)(2,1)} %get-tuple-element.283, s32[]{:T(128)} %get-tuple-element.280, bf16[16,2,1504,328]{3,2,1,0:T(8,128)(2,1)} %get-tuple-element.286, s32[]{:T(128)} %bitcast.75), kind=kLoop, calls=%fused_computation.10.clone.1 | loop fusion | bytes 24642560 | tf_op jit(solution)/shard_map/while/body/eval_jaxpr/vmap()/gather
  906.2 33.2 %fusion.55 = (bf16[5,1504,128]{2,1,0:T(8,128)(2,1)}, bf16[5,1504,128]{2,1,0:T(8,128)(2,1)}) fusion(f32[16,1504,128]{2,1,0:T(8,128)S(1)} %get-tuple-element.265, f32[16,1504,128]{2,1,0:T(8,128)S(1)} %get-tuple-element.266, bf16[5,16,2,1504,128]{4,3,2,1,0:T(8,128)(2,1)} %get-tuple-element.267), kind=kLoop, calls=%fused_computation.17.clone.1 | loop fusion | flops 152084480 | bytes 90095616 | tf_op jit(solution)/shard_map/while/body/eval_jaxpr/reduce_sum | solution.py:56
  944.8 77.7 %while.27 = (s32[]{:T(128)}, bf16[16,2,1504,328]{3,2,1,0:T(8,128)(2,1)}, s32[5,4]{0,1:T(4,128)S(1)}, bf16[5,16,2,1504,128]{4,3,2,1,0:T(8,128)(2,1)}, s32[]{:T(128)}) while((s32[]{:T(128)}, bf16[16,2,1504,328]{3,2,1,0:T(8,128)(2,1)}, s32[5,4]{0,1:T(4,128)S(1)}, bf16[5,16,2,1504,128]{4,3,2,1,0:T(8,128)(2,1)}, s32[]{:T(128)}) %tuple.62), condition=%wide.while_cond, body=%wide.while_body.sunk | while | flops 2 | bytes 24642664 | solution.py:72
  945.5 14.9 %bitcast_dynamic-update-slice_fusion.2 = bf16[5,16,2,1504,128]{4,3,2,1,0:T(8,128)(2,1)} fusion(bf16[5,16,2,1504,128]{4,3,2,1,0:T(8,128)(2,1)} %get-tuple-element.283, s32[]{:T(128)} %get-tuple-element.280, bf16[16,2,1504,328]{3,2,1,0:T(8,128)(2,1)} %get-tuple-element.286, s32[]{:T(128)} %bitcast.75), kind=kLoop, calls=%fused_computation.10.clone.1 | loop fusion | bytes 24642560 | tf_op jit(solution)/shard_map/while/body/eval_jaxpr/vmap()/gather
  1028.9 33.2 %fusion.55 = (bf16[5,1504,128]{2,1,0:T(8,128)(2,1)}, bf16[5,1504,128]{2,1,0:T(8,128)(2,1)}) fusion(f32[16,1504,128]{2,1,0:T(8,128)S(1)} %get-tuple-element.265, f32[16,1504,128]{2,1,0:T(8,128)S(1)} %get-tuple-element.266, bf16[5,16,2,1504,128]{4,3,2,1,0:T(8,128)(2,1)} %get-tuple-element.267), kind=kLoop, calls=%fused_computation.17.clone.1 | loop fusion | flops 152084480 | bytes 90095616 | tf_op jit(solution)/shard_map/while/body/eval_jaxpr/reduce_sum | solution.py:56
  1067.5 77.7 %while.27 = (s32[]{:T(128)}, bf16[16,2,1504,328]{3,2,1,0:T(8,128)(2,1)}, s32[5,4]{0,1:T(4,128)S(1)}, bf16[5,16,2,1504,128]{4,3,2,1,0:T(8,128)(2,1)}, s32[]{:T(128)}) while((s32[]{:T(128)}, bf16[16,2,1504,328]{3,2,1,0:T(8,128)(2,1)}, s32[5,4]{0,1:T(4,128)S(1)}, bf16[5,16,2,1504,128]{4,3,2,1,0:T(8,128)(2,1)}, s32[]{:T(128)}) %tuple.62), condition=%wide.while_cond, body=%wide.while_body.sunk | while | flops 2 | bytes 24642664 | solution.py:72
  1068.1 14.9 %bitcast_dynamic-update-slice_fusion.2 = bf16[5,16,2,1504,128]{4,3,2,1,0:T(8,128)(2,1)} fusion(bf16[5,16,2,1504,128]{4,3,2,1,0:T(8,128)(2,1)} %get-tuple-element.283, s32[]{:T(128)} %get-tuple-element.280, bf16[16,2,1504,328]{3,2,1,0:T(8,128)(2,1)} %get-tuple-element.286, s32[]{:T(128)} %bitcast.75), kind=kLoop, calls=%fused_computation.10.clone.1 | loop fusion | bytes 24642560 | tf_op jit(solution)/shard_map/while/body/eval_jaxpr/vmap()/gather
  1151.6 33.2 %fusion.55 = (bf16[5,1504,128]{2,1,0:T(8,128)(2,1)}, bf16[5,1504,128]{2,1,0:T(8,128)(2,1)}) fusion(f32[16,1504,128]{2,1,0:T(8,128)S(1)} %get-tuple-element.265, f32[16,1504,128]{2,1,0:T(8,128)S(1)} %get-tuple-element.266, bf16[5,16,2,1504,128]{4,3,2,1,0:T(8,128)(2,1)} %get-tuple-element.267), kind=kLoop, calls=%fused_computation.17.clone.1 | loop fusion | flops 152084480 | bytes 90095616 | tf_op jit(solution)/shard_map/while/body/eval_jaxpr/reduce_sum | solution.py:56
  1190.2 77.7 %while.27 = (s32[]{:T(128)}, bf16[16,2,1504,328]{3,2,1,0:T(8,128)(2,1)}, s32[5,4]{0,1:T(4,128)S(1)}, bf16[5,16,2,1504,128]{4,3,2,1,0:T(8,128)(2,1)}, s32[]{:T(128)}) while((s32[]{:T(128)}, bf16[16,2,1504,328]{3,2,1,0:T(8,128)(2,1)}, s32[5,4]{0,1:T(4,128)S(1)}, bf16[5,16,2,1504,128]{4,3,2,1,0:T(8,128)(2,1)}, s32[]{:T(128)}) %tuple.62), condition=%wide.while_cond, body=%wide.while_body.sunk | while | flops 2 | bytes 24642664 | solution.py:72
  1190.8 14.9 %bitcast_dynamic-update-slice_fusion.2 = bf16[5,16,2,1504,128]{4,3,2,1,0:T(8,128)(2,1)} fusion(bf16[5,16,2,1504,128]{4,3,2,1,0:T(8,128)(2,1)} %get-tuple-element.283, s32[]{:T(128)} %get-tuple-element.280, bf16[16,2,1504,328]{3,2,1,0:T(8,128)(2,1)} %get-tuple-element.286, s32[]{:T(128)} %bitcast.75), kind=kLoop, calls=%fused_computation.10.clone.1 | loop fusion | bytes 24642560 | tf_op jit(solution)/shard_map/while/body/eval_jaxpr/vmap()/gather
  1274.2 33.2 %fusion.55 = (bf16[5,1504,128]{2,1,0:T(8,128)(2,1)}, bf16[5,1504,128]{2,1,0:T(8,128)(2,1)}) fusion(f32[16,1504,128]{2,1,0:T(8,128)S(1)} %get-tuple-element.265, f32[16,1504,128]{2,1,0:T(8,128)S(1)} %get-tuple-element.266, bf16[5,16,2,1504,128]{4,3,2,1,0:T(8,128)(2,1)} %get-tuple-element.267), kind=kLoop, calls=%fused_computation.17.clone.1 | loop fusion | flops 152084480 | bytes 90095616 | tf_op jit(solution)/shard_map/while/body/eval_jaxpr/reduce_sum | solution.py:56
  (141 shorter events, 395.6 us)
Async XLA Ops:
  6.5 251.1 %all-gather.2.cloned.1.call-start = ((), (), s32[]{:S(2)}) async-start(), calls=%async_computation | async-start | bytes 13860864 | tf_op jit(solution)/shard_map/all_gather | solution.py:104
  85.3 15.7 %copy-start.1 = (s32[2]{0:T(128)S(1)}, s32[2]{0:T(128)}, u32[]{:S(2)}) copy-start(s32[2]{0:T(128)} %param.7) | copy-start | bytes 28
  125.4 1.1 copy-start
  268.0 265.5 %collective-permute-start = (bf16[16,2,1504,128]{3,2,1,0:T(8,128)(2,1)}, bf16[16,2,1504,128]{3,2,1,0:T(8,128)(2,1)}, u32[]{:S(2)}, u32[]{:S(2)}) collective-permute-start(bf16[16,2,1504,128]{3,2,1,0:T(8,128)(2,1)} %copy.7), channel_id=1, source_target_pairs={{1,0},{2,1},{3,2},{4,3},{5,4},{6,5},{7,6},{8,7},{9,8},{10,9},{11,1... | collective-permute-start | bytes 36962312 | tf_op jit(solution)/shard_map/ppermute | solution.py:17
  270.2 402.7 %collective-permute-start.1 = (bf16[16,2,1504,128]{3,2,1,0:T(8,128)(2,1)}, bf16[16,2,1504,128]{3,2,1,0:T(8,128)(2,1)}, u32[]{:S(2)}, u32[]{:S(2)}) collective-permute-start(bf16[16,2,1504,128]{3,2,1,0:T(8,128)(2,1)} %copy.7), channel_id=1, source_target_pairs={{2,0},{3,1},{4,2},{5,3},{6,4},{7,5},{8,6},{9,7},{10,8},{11,9},{12,... | collective-permute-start | bytes 36962312 | tf_op jit(solution)/shard_map/ppermute | solution.py:17
Sparse Core Ops, SparseCore 0:
  126.7 130.8 all-gather.1
where the time goes:
time: 1320 us
  waiting for transfers between devices  527 us (40%)
  local copies, waits for them, and re-layouts  404 us (31%)
  other arithmetic  323 us (24%)
  matrix products  38.5 us (3%)
  between operations  13.5 us (1%)
    ppermute x2, waiting for transfers between devices, from_behind(): return lax.ppermute(block, axis, route)  396 us
    gather x75, local copies, waits for them, and re-layouts  388 us
    reduce_sum x5, other arithmetic, conj_sum(): real = jnp.sum(real_own * real_far + imag_own * imag_far, axis=-3)  166 us
    all_gather x1, waiting for transfers between devices, body(): every = lax.all_gather(white, 'tm', axis=0, tiled=True)  131 us
    another operation x2, other arithmetic  82.4 us
    convert_element_type x5, other arithmetic, conj_sum(): real_own = own[..., 0, :, :].astype(jnp.float32)  32.2 us
  transfers between devices with their start and end apart: 3, of which 3 were waited for; matrix products, arithmetic and copies ran while one was open for 0% of the time, Pallas kernels for 0%

commit v1 on v0

v1 whole, which is shorter than its diff:
```python
import math

import jax
import jax.numpy as jnp
import ml_dtypes
import numpy as np
from jax import lax
from jax.experimental import pallas as pl
from jax.experimental.pallas import tpu as pltpu
from jax.sharding import PartitionSpec as P

SAMP = 3000
F = 1501
ROWS = 1504
BAND = 200
LAGS = 128
HALF = LAGS // 2
SEG = 64
SLOTS = 48
SPAN = 192
POINTS = 191
BINS = 96
BF16 = ml_dtypes.bfloat16


def turns(a, b, period):
    return 2.0 * math.pi * (np.outer(a, b) % period) / period


def dft_table():
    angle = turns(np.arange(F), np.arange(SAMP), SAMP)
    table = np.zeros((2, ROWS, SAMP), np.float32)
    table[0, :F] = np.cos(angle) / math.sqrt(SAMP)
    table[1, :F] = -np.sin(angle) / math.sqrt(SAMP)
    return table.reshape(2 * ROWS, SAMP).astype(BF16)


def inverse_table(rows):
    time = (np.arange(rows) - HALF) % SAMP
    weight = np.full(F, 2.0)
    weight[0] = weight[-1] = 1.0
    angle = turns(time, np.arange(F), SAMP)
    table = np.zeros((rows, 2, ROWS), np.float32)
    table[:, 0, :F] = weight * np.cos(angle) / math.sqrt(SAMP)
    table[:, 1, :F] = -weight * np.sin(angle) / math.sqrt(SAMP)
    return table.reshape(rows, 2 * ROWS).astype(BF16)


def segment_tables():
    angle = turns(np.arange(BINS), np.arange(SPAN), POINTS)
    full = np.concatenate([np.cos(angle), -np.sin(angle)]) / math.sqrt(POINTS)
    full[:, POINTS:] = 0.0
    high = full.astype(BF16)
    low = (full - high.astype(np.float64)).astype(BF16)
    return high, np.concatenate([high[:, :SEG], low[:, :SEG]], axis=1)


def lag_table(windows):
    angle = turns(np.arange(BINS), np.arange(LAGS), POINTS)
    weight = np.full((BINS, 1), 2.0)
    weight[0] = 1.0
    table = np.stack([weight * np.cos(angle), -weight * np.sin(angle)], axis=1)
    return (table / math.sqrt(SAMP * windows)).reshape(2 * BINS, LAGS).astype(BF16)


def whiten(spec):
    parts = spec.reshape(2, ROWS, spec.shape[1])
    power = parts[0] * parts[0] + parts[1] * parts[1]
    padded = jnp.pad(power, ((1, 1), (0, 0)))
    smooth = (padded[:-2] + power + padded[2:]) / 3.0
    factor = 1.0 / jnp.maximum(jnp.sqrt(smooth), 0.5)
    return (parts * factor[None]).astype(jnp.bfloat16)


FIRST = 7
OUT_ROWS = FIRST + BAND + 8


def pair_kernel(ya, yd, fa, fd, lag, out, sega, bins, gram, rows):
    width = yd.shape[2] // 2

    def long_segment(s, carry):
        block = ya[pl.ds(pl.multiple_of(s * SEG, SEG), SPAN), :]
        spec = jnp.dot(fa[...], block, preferred_element_type=jnp.float32)
        bins[0, pl.ds(s, 2 * BINS, stride=SLOTS), :] = spec[:, :width]
        bins[1, pl.ds(s, 2 * BINS, stride=SLOTS), :] = spec[:, width:]
        return carry

    lax.fori_loop(0, SLOTS - 1, long_segment, 0)
    zero = jnp.zeros((2 * BINS, width), jnp.float32)
    bins[0, pl.ds(SLOTS - 1, 2 * BINS, stride=SLOTS), :] = zero
    bins[1, pl.ds(SLOTS - 1, 2 * BINS, stride=SLOTS), :] = zero

    def of_bin(b):
        real = pl.ds(pl.multiple_of(b * SLOTS, SLOTS), SLOTS)
        imag = pl.ds(pl.multiple_of((b + BINS) * SLOTS, SLOTS), SLOTS)
        return [bins[0, real, :], bins[1, real, :], bins[0, imag, :], bins[1, imag, :]]

    def turn_bin(b, carry):
        r0, r1, i0, i1 = of_bin(b)
        sega[b, :width, :] = jnp.concatenate([r0, r1, i0, i1], 0).T.astype(jnp.bfloat16)
        sega[b, width:, :] = jnp.concatenate([i0, i1, -r0, -r1], 0).T.astype(jnp.bfloat16)
        return carry

    lax.fori_loop(0, BINS, turn_bin, 0)

    for q in range(yd.shape[0]):

        def short_segment(s, carry):
            block = yd[q, pl.ds(pl.multiple_of(s * SEG, SEG), SEG), :]
            twice = jnp.concatenate([block, block], 0)
            spec = jnp.dot(fd[...], twice, preferred_element_type=jnp.float32)
            bins[0, pl.ds(s, 2 * BINS, stride=SLOTS), :] = spec[:, :width]
            bins[1, pl.ds(s, 2 * BINS, stride=SLOTS), :] = spec[:, width:]
            return carry

        lax.fori_loop(0, SLOTS, short_segment, 0)

        def one_bin(b, carry):
            far = jnp.concatenate(of_bin(b), 0).astype(jnp.bfloat16)
            cross = jnp.dot(sega[b], far, preferred_element_type=jnp.float32)
            gram[pl.ds(pl.multiple_of(b * 2 * width, 2 * width), 2 * width), :] = cross
            return carry

        lax.fori_loop(0, BINS, one_bin, 0)

        def one_channel(c, carry):
            cross = gram[pl.ds(c, 2 * BINS, stride=width), :].astype(jnp.bfloat16)
            lags = lax.dot_general(
                cross, lag[...], (((0,), (0,)), ((), ())), preferred_element_type=jnp.float32
            )
            for i in range(width // 8):
                k = q * width + 8 * i - c

                @pl.when((k > -8) & (k <= BAND))
                def _():
                    first = (k + FIRST) * width + c
                    rows[pl.ds(first, 8, stride=width), :] = lags[8 * i : 8 * i + 8]

            return carry

        lax.fori_loop(0, width, one_channel, 0)

    def finish(k, carry):
        first = pl.multiple_of((k + FIRST + 1) * width, width)
        out[k] = rows[pl.ds(first, width), :].astype(jnp.bfloat16)
        return carry

    lax.fori_loop(0, BAND, finish, 0)


def correlate(ya, yd, windows):
    width = yd.shape[2] // 2
    fa, fd = segment_tables()
    vmem = pl.BlockSpec(memory_space=pltpu.VMEM)
    return pl.pallas_call(
        pair_kernel,
        out_shape=jax.ShapeDtypeStruct((BAND, width, LAGS), jnp.bfloat16),
        in_specs=[vmem] * 5,
        out_specs=vmem,
        scratch_shapes=[
            pltpu.VMEM((BINS, 2 * width, 4 * SLOTS), jnp.bfloat16),
            pltpu.VMEM((2, 2 * BINS * SLOTS, width), jnp.float32),
            pltpu.VMEM((2 * BINS * width, width), jnp.float32),
            pltpu.VMEM((OUT_ROWS * width, LAGS), jnp.float32),
        ],
        compiler_params=pltpu.CompilerParams(vmem_limit_bytes=62 * 2**20),
        cost_estimate=pl.CostEstimate(flops=6 * 10**9, bytes_accessed=20 * 10**6, transcendentals=0),
    )(ya, yd, jnp.asarray(fa), jnp.asarray(fd), jnp.asarray(lag_table(windows)))


def time_series(record, starts):
    samples = jnp.concatenate(
        [lax.dynamic_slice_in_dim(record, starts[w], SAMP, 0) for w in range(starts.shape[0])], 1
    )
    spec = jnp.dot(jnp.asarray(dft_table()), samples, preferred_element_type=jnp.float32)
    white = whiten(spec).reshape(2 * ROWS, samples.shape[1])
    table = jnp.asarray(inverse_table(SEG * (SLOTS + 2)))
    return jnp.dot(table, white, preferred_element_type=jnp.float32).astype(jnp.bfloat16)


def body(record, starts):
    groups = lax.axis_size("tm")
    blocks = lax.axis_size("chan")
    ya = time_series(record, starts)
    own = jnp.pad(ya[HALF : HALF + SAMP], ((0, SEG * SLOTS - SAMP), (0, 0)))
    after = lax.ppermute(own, "chan", [(j, j - 1) for j in range(1, blocks)])
    beyond = lax.ppermute(own, "chan", [(j, j - 2) for j in range(2, blocks)])
    yd = jnp.stack([own, after, beyond])
    part = correlate(ya, yd, starts.shape[0] * groups)
    total = lax.psum_scatter(part, "tm", scatter_dimension=0, tiled=True)
    return total.astype(jnp.float32)


def solution(mesh):
    return jax.shard_map(
        body,
        mesh=mesh,
        in_specs=(P("tm", "chan"), P("tm")),
        out_specs=P("tm", "chan", None),
        check_vma=False,
    )
```

time: 1320 us -> 437 us (0.33)
  the two profiles are of different devices: /device:TPU:24 before, /device:TPU:25 now
where the time goes in v1:
time: 437 us; the launch traced here: 436 us
  Pallas kernels  257 us (59%)
  waiting for transfers between devices  130 us (30%)
  between operations  17.4 us (4%)
  matrix products  15.1 us (3%)
  other arithmetic  6.47 us (1%)
  local copies, waits for them, and re-layouts  5.6 us (1%)
  starting transfers between devices  4.95 us (1%)
    pallas_call x1, Pallas kernels, correlate(): pl.pallas_call(pair_kernel, out_shape=jax.ShapeDtypeStruct((BAND, width,...  257 us
    reduce_scatter x1, waiting for transfers between devices, body(): total = lax.psum_scatter(part, 'tm', scatter_dimension=0, tiled=True)  90 us
    ppermute x1, waiting for transfers between devices, body(): after = lax.ppermute(own, 'chan', [(j, j - 1) for j in range(1, blocks)])  35.1 us
    dot_general x1, matrix products, time_series(): jnp.dot(jnp.asarray(dft_table()), samples, preferred_element_type=jnp.flo...  9.2 us
  transfers between devices with their start and end apart: 3, of which 3 were waited for; matrix products, arithmetic and copies ran while one was open for 0% of the time, Pallas kernels for 0%

profile of v1, /device:TPU:25, one launch (start us, length us, event | category | flops | bytes accessed | tf_op | source)
XLA Modules:
  0.0 436.0 jit_solution(2815809879371163248)
XLA Ops:
  6.5 1.3 fusion.5
  11.7 1.8 constant_dynamic-slice_fusion.1
  13.5 0.0 slice-start
  13.5 0.0 slice-start.1
  13.5 0.0 slice-start.2
  13.5 0.0 slice-start.3
  13.5 9.2 %fusion.3 = f32[3008,256]{1,0:T(8,128)S(1)} fusion(bf16[3008,3000]{1,0:T(8,128)(2,1)} %constant.25.clone, bf16[3000,128]{1,0:T(8,128)(2,1)S(1)} %get-tuple-element.6, bf16[3000,128]{1,0:T(8,128)(2,1)S(1)} %get-tuple-element.5), kind=kOutput, calls=%fused_computation.10 | convolution fusion | flops 4623360000 | bytes 22664192 | tf_op jit(solution)/shard_map/dot_general | solution.py:176
  22.8 0.2 fusion.2
  23.0 0.8 maximum_divide_fusion
  23.8 0.5 fusion.1
  24.3 1.3 slice-done.4
  25.7 5.9 %fusion.ya = bf16[3200,256]{1,0:T(8,128)(2,1)S(1)} fusion(bf16[3200,3008]{1,0:T(8,128)(2,1)S(1)} %bitcast.18, bf16[3008,256]{1,0:T(8,128)(2,1)S(1)} %fusion.1), kind=kOutput, calls=%fused_computation.1 | convolution fusion | flops 4929126400 | bytes 22429696 | tf_op jit(solution)/shard_map/dot_general | solution.py:179
  31.6 0.1 slice.34
  31.7 0.2 pad_bitcast_fusion
  31.9 0.8 copy-done
  32.8 2.6 collective-permute-start
  35.4 2.4 collective-permute-start.1
  37.7 35.1 %collective-permute-done = bf16[3072,256]{1,0:T(8,128)(2,1)S(1)} collective-permute-done((bf16[3072,256]{1,0:T(8,128)(2,1)S(1)}, bf16[3072,256]{1,0:T(8,128)(2,1)S(1)}, u32[]{:S(2)}, u32[]{:S(2)}) %collective-permute-start) | collective-permute-done | bytes 1572896 | tf_op jit(solution)/shard_map/ppermute | solution.py:187
  72.9 4.5 %collective-permute-done.1 = bf16[3072,256]{1,0:T(8,128)(2,1)S(1)} collective-permute-done((bf16[3072,256]{1,0:T(8,128)(2,1)S(1)}, bf16[3072,256]{1,0:T(8,128)(2,1)S(1)}, u32[]{:S(2)}, u32[]{:S(2)}) %collective-permute-start.1) | collective-permute-done | bytes 1572896 | tf_op jit(solution)/shard_map/ppermute | solution.py:188
  77.3 2.5 pad_maximum_fusion.yd
  79.8 256.9 %shard_map.73 = bf16[200,128,128]{2,1,0:T(8,128)(2,1)} custom-call(bf16[3200,256]{1,0:T(8,128)(2,1)} %copy-done, bf16[3,3072,256]{2,1,0:T(8,128)(2,1)} %pad_maximum_fusion.yd, bf16[192,192]{1,0:T(8,128)(2,1)} %constant.27.clone.fa, bf16[192,128]{1,0:T(8,128)(2,1)} %constant.28.clone.fd, bf16[192,128]{1,0:T(8,128)(2,1)} %constant.29.clone.lag), custom_call_target="tpu_custom_call" | custom-call | flops 6000000000 | bytes 20000000 | tf_op jit(solution)/shard_map/pallas_call | solution.py:156
  336.7 0.0 reduce-scatter.2.cloned.1.call-update
  336.7 90.0 %reduce-scatter.2.cloned.1.call-done = bf16[25,128,128]{2,1,0:T(8,128)(2,1)} async-done(((bf16[200,128,128]{2,1,0:T(8,128)(2,1)}), bf16[25,128,128]{2,1,0:T(8,128)(2,1)}) %reduce-scatter.2.cloned.1.call-update) | async-done | bytes 819216 | tf_op jit(solution)/shard_map/reduce_scatter | solution.py:191
  426.7 2.5 convert_element_type.19
  (8 shorter events, 0.0 us)
Async XLA Ops:
  6.5 420.2 %reduce-scatter.2.cloned.1.call-start = ((), (), s32[]{:S(2)}) async-start(), calls=%async_computation.1 | async-start | bytes 7372800 | tf_op jit(solution)/shard_map/reduce_scatter | solution.py:191
  13.5 10.8 %slice-start = ((s8[19660800]{0:T(1024)(128)(4,1)}), s8[4194304]{0:T(1024)(128)(4,1)S(1)}, s32[]{:S(2)}) async-start(s8[19660800]{0:T(1024)(128)(4,1)} %bitcast.17), calls=%async_computation.2 | async-start | bytes 8388608
  13.5 10.8 %slice-start.1 = ((s8[19660800]{0:T(1024)(128)(4,1)}), s8[4194304]{0:T(1024)(128)(4,1)S(1)}, s32[]{:S(2)}) async-start(s8[19660800]{0:T(1024)(128)(4,1)} %bitcast.17), calls=%async_computation.3 | async-start | bytes 8388608
  13.5 10.8 %slice-start.2 = ((s8[19660800]{0:T(1024)(128)(4,1)}), s8[4194304]{0:T(1024)(128)(4,1)S(1)}, s32[]{:S(2)}) async-start(s8[19660800]{0:T(1024)(128)(4,1)} %bitcast.17), calls=%async_computation.4 | async-start | bytes 8388608
  13.5 10.8 %slice-start.3 = ((s8[19660800]{0:T(1024)(128)(4,1)}), s8[2883584]{0:T(1024)(128)(4,1)S(1)}, s32[]{:S(2)}) async-start(s8[19660800]{0:T(1024)(128)(4,1)} %bitcast.17), calls=%async_computation.5 | async-start | bytes 5767168
  22.8 2.9 slice-start.4
  31.6 1.2 copy-start
  32.8 40.1 %collective-permute-start = (bf16[3072,256]{1,0:T(8,128)(2,1)S(1)}, bf16[3072,256]{1,0:T(8,128)(2,1)S(1)}, u32[]{:S(2)}, u32[]{:S(2)}) collective-permute-start(bf16[3072,256]{1,0:T(8,128)(2,1)S(1)} %get-tuple-element.8), channel_id=1, source_target_pairs={{1,0},{2,1},{3,2},{4,3},{5,4},{6,5},{7,6},{8,7},{9,8},{10,9},{11,1... | collective-permute-start | bytes 4718600 | tf_op jit(solution)/shard_map/ppermute | solution.py:187
  35.4 42.0 %collective-permute-start.1 = (bf16[3072,256]{1,0:T(8,128)(2,1)S(1)}, bf16[3072,256]{1,0:T(8,128)(2,1)S(1)}, u32[]{:S(2)}, u32[]{:S(2)}) collective-permute-start(bf16[3072,256]{1,0:T(8,128)(2,1)S(1)} %get-tuple-element.8), channel_id=1, source_target_pairs={{2,0},{3,1},{4,2},{5,3},{6,4},{7,5},{8,6},{9,7},{10,8},{11,9},{12,... | collective-permute-start | bytes 4718600 | tf_op jit(solution)/shard_map/ppermute | solution.py:188
Sparse Core Ops, SparseCore 0:
  336.9 89.8 reduce-scatter.1

commit v2 on v1

v2 whole, which is shorter than its diff:
```python
import math

import jax
import jax.numpy as jnp
import ml_dtypes
import numpy as np
from jax import lax
from jax.experimental import pallas as pl
from jax.experimental.pallas import tpu as pltpu
from jax.sharding import PartitionSpec as P

SAMP = 3000
F = 1501
ROWS = 1504
BAND = 200
LAGS = 128
HALF = LAGS // 2
SEG = 64
SLOTS = 48
SPAN = 192
POINTS = 191
BINS = 96
BF16 = ml_dtypes.bfloat16


def turns(a, b, period):
    return 2.0 * math.pi * (np.outer(a, b) % period) / period


def dft_table():
    angle = turns(np.arange(F), np.arange(SAMP), SAMP)
    table = np.zeros((2, ROWS, SAMP), np.float32)
    table[0, :F] = np.cos(angle) / math.sqrt(SAMP)
    table[1, :F] = -np.sin(angle) / math.sqrt(SAMP)
    return table.reshape(2 * ROWS, SAMP).astype(BF16)


def inverse_table(rows):
    time = (np.arange(rows) - HALF) % SAMP
    weight = np.full(F, 2.0)
    weight[0] = weight[-1] = 1.0
    angle = turns(time, np.arange(F), SAMP)
    table = np.zeros((rows, 2, ROWS), np.float32)
    table[:, 0, :F] = weight * np.cos(angle) / math.sqrt(SAMP)
    table[:, 1, :F] = -weight * np.sin(angle) / math.sqrt(SAMP)
    return table.reshape(rows, 2 * ROWS).astype(BF16)


def segment_tables():
    angle = turns(np.arange(BINS), np.arange(SPAN), POINTS)
    full = np.stack([np.cos(angle), -np.sin(angle)], axis=1) / math.sqrt(POINTS)
    full = full.reshape(2 * BINS, SPAN)
    full[:, POINTS:] = 0.0
    high = full.astype(BF16)
    low = (full - high.astype(np.float64)).astype(BF16)
    return high, np.concatenate([high[:, :SEG], low[:, :SEG]], axis=1)


def lag_table(windows):
    angle = turns(np.arange(BINS), np.arange(LAGS), POINTS)
    weight = np.full((BINS, 1), 2.0)
    weight[0] = 1.0
    table = np.stack([weight * np.cos(angle), -weight * np.sin(angle)], axis=1)
    return (table / math.sqrt(SAMP * windows)).reshape(2 * BINS, LAGS).astype(BF16)


def whiten(spec):
    parts = spec.reshape(2, ROWS, spec.shape[1])
    power = parts[0] * parts[0] + parts[1] * parts[1]
    padded = jnp.pad(power, ((1, 1), (0, 0)))
    smooth = (padded[:-2] + power + padded[2:]) / 3.0
    factor = 1.0 / jnp.maximum(jnp.sqrt(smooth), 0.5)
    return (parts * factor[None]).astype(jnp.bfloat16)


FIRST = 8
OUT_ROWS = FIRST + BAND + 9
HELD = 2 * 2 * SLOTS
CHUNK = 16
RING = 4
LIVE = 4
MESH = pl.DeviceIdType.MESH


def unrolled(count, step, times):
    def several(i, carry):
        step([i * times + u for u in range(times)])
        return carry

    lax.fori_loop(0, count // times, several, 0)


def pair_kernel(
    ya, own, fa, fd, lag, out,
    sega, bins, gram, rows, near, far, part, hop, land, across,
    sent, come, sent_y, come_y,
):
    width = own.shape[1] // 2
    share = out.shape[0]
    chunks = width // CHUNK
    blocks = lax.axis_size("chan")
    i, j = lax.axis_index("tm"), lax.axis_index("chan")
    x, z = lax.rem(i, RING), i // RING
    right = {"tm": z * RING + lax.rem(x + 1, RING)}
    left = {"tm": z * RING + lax.rem(x + RING - 1, RING)}
    other = {"tm": (1 - z) * RING + x}
    odd = lax.rem(j, 2) == 1

    def behind(distance):
        return {"chan": lax.rem(j + blocks + distance, blocks)}

    barrier = pltpu.get_barrier_semaphore()
    peers = (right, left, other, behind(-1), behind(1), behind(-2), behind(2))
    for device in peers:
        pl.semaphore_signal(barrier, inc=1, device_id=device, device_id_type=MESH)
    pl.semaphore_wait(barrier, len(peers))

    def remote(source, target, send, receive, device):
        return pltpu.make_async_remote_copy(
            src_ref=source, dst_ref=target, send_sem=send, recv_sem=receive,
            device_id=device, device_id_type=MESH,
        )

    to_near = remote(own, near, sent_y.at[0], come_y.at[0], behind(-1))
    to_far = remote(own, far, sent_y.at[1], come_y.at[1], behind(-2))
    pass_on = remote(near, far, sent_y.at[2], come_y.at[1], behind(-1))
    to_near.start()

    @pl.when(odd)
    def _():
        to_far.start()

    def spread(slot, s, spec):
        at = slot * 2 * SLOTS + s
        bins[pl.ds(at, 2 * BINS, stride=HELD), :] = spec[:, :width]
        bins[pl.ds(at + SLOTS, 2 * BINS, stride=HELD), :] = spec[:, width:]

    def long_segments(index):
        specs = []
        for s in index:
            block = ya[pl.ds(pl.multiple_of(s * SEG, SEG), SPAN), :]
            specs.append(jnp.dot(fa[...], block, preferred_element_type=jnp.float32))
        for s, spec in zip(index, specs):
            spread(0, s, spec)

    def short_segments(source, slot, holds):
        table = fd[...]
        if holds is not None:
            table = jnp.where(holds, table, jnp.zeros_like(table))

        def step(index):
            specs = []
            for s in index:
                block = source[pl.ds(pl.multiple_of(s * SEG, SEG), SEG), :]
                twice = jnp.concatenate([block, block], 0)
                specs.append(jnp.dot(table, twice, preferred_element_type=jnp.float32))
            for s, spec in zip(index, specs):
                spread(slot, s, spec)

        unrolled(SLOTS, step, 8)

    def of_bin(slot, b):
        first = pl.multiple_of(b * 2 * HELD, 2 * HELD) + slot * 2 * SLOTS
        return bins[pl.ds(first, 2 * SLOTS), :], bins[pl.ds(first + HELD, 2 * SLOTS), :]

    def turn_bins(index):
        for b in index:
            sega[b] = jnp.concatenate(of_bin(0, b), 0).T.astype(jnp.bfloat16)

    def product(slot, b):
        real, imag = [part.astype(jnp.bfloat16) for part in of_bin(slot, b)]
        both = jnp.concatenate(
            [jnp.concatenate([real, imag], 0), jnp.concatenate([-imag, real], 0)], 1
        )
        return jnp.dot(sega[b], both, preferred_element_type=jnp.float32)

    def keep(target, pitch, b, cross):
        first = pl.multiple_of(b * 2 * pitch, 2 * pitch)
        target[pl.ds(first, width), :] = cross[:, :width]
        target[pl.ds(first + pitch, width), :] = cross[:, width:]

    def gram_next(index):
        for b, cross in zip(index, [product(1, b) for b in index]):
            keep(gram, width, b, cross)

    same = lax.broadcasted_iota(jnp.int32, (width, 2 * width), 1) % width
    same = same > lax.broadcasted_iota(jnp.int32, (width, 2 * width), 0)

    def gram_own(index):
        crosses = [jnp.where(same, product(0, b), product(1, b)) for b in index]
        for b, cross in zip(index, crosses):
            keep(bins, HELD, b, cross)

    def place_next(ahead, c):
        return width + ahead - c

    def place_own(ahead, c):
        return jnp.where(ahead + 7 > c, ahead - c, 2 * width + ahead - c)

    def lag_step(source, pitch, place, base):
        def step(index):
            cross = jnp.concatenate(
                [
                    source[pl.ds(base + c, 2 * BINS, stride=pitch), :].astype(jnp.bfloat16)
                    for c in index
                ],
                1,
            )
            lags = lax.dot_general(
                cross, lag[...], (((0,), (0,)), ((), ())), preferred_element_type=jnp.float32
            )
            for u, c in enumerate(index):
                for e in range(width // 8):
                    k = jnp.clip(place(8 * e, base + c), -FIRST, BAND + 1)
                    at = u * width + 8 * e
                    rows[pl.ds((k + FIRST) * CHUNK + c, 8, stride=CHUNK), :] = lags[at : at + 8]

        return step

    unrolled(SLOTS, long_segments, 8)
    unrolled(BINS, turn_bins, 8)
    short_segments(own, 0, None)
    to_near.wait_recv()

    @pl.when(odd)
    def _():
        pass_on.start()

    short_segments(near, 1, j < blocks - 1)
    unrolled(BINS, gram_next, 8)
    to_far.wait_recv()
    short_segments(far, 1, j < blocks - 2)
    unrolled(BINS, gram_own, 8)

    def at(column, row):
        return row * RING + lax.rem(column + RING, RING)

    def message(n, m):
        slot = n % LIVE
        source, target, device = [
            (part.at[slot, at(x + 2, 0)], hop.at[n, 0], right),
            (part.at[slot, at(x + 2, 1)], hop.at[n, 1], left),
            (part.at[slot, at(x + 1, 1)], land.at[n, 0, 1], right),
            (part.at[slot, at(x - 1, 0)], land.at[n, 1, 0], left),
            (part.at[slot, at(x + 1, 0)], land.at[n, 0, 0], right),
            (part.at[slot, at(x - 1, 1)], land.at[n, 1, 1], left),
            (part.at[slot, at(x, 1 - z)], across.at[n], other),
        ][m]
        return remote(source, target, sent.at[n, m], come.at[n, m], device)

    def plus(n, place, others):
        slot = n % LIVE

        def step(k, carry):
            total = part[slot, place, k].astype(jnp.float32)
            for ref in others:
                total += ref[k].astype(jnp.float32)
            part[slot, place, k] = total.astype(jnp.bfloat16)
            return carry

        lax.fori_loop(0, share, step, 0)

    def begin(n):
        unrolled(CHUNK, lag_step(gram, width, place_next, n * CHUNK), 8)
        unrolled(CHUNK, lag_step(bins, HELD, place_own, n * CHUNK), 8)
        slot = n % LIVE

        def step(k, carry):
            for d in range(BAND // share):
                first = pl.multiple_of((d * share + k + FIRST + 1) * CHUNK, CHUNK)
                part[slot, d, k] = rows[pl.ds(first, CHUNK), :].astype(jnp.bfloat16)
            return carry

        lax.fori_loop(0, share, step, 0)
        for m in range(4):
            message(n, m).start()

    def second(n):
        for m in range(2):
            message(n, m).wait_recv()
        plus(n, at(x + 1, 0), [hop.at[n, 0]])
        message(n, 4).start()
        plus(n, at(x - 1, 1), [hop.at[n, 1]])
        message(n, 5).start()

    def third(n):
        for m in range(2, 6):
            message(n, m).wait_recv()
        plus(n, at(x, 1 - z), [land.at[n, 0, 1 - z], land.at[n, 1, 1 - z]])
        message(n, 6).start()

    def last(n):
        message(n, 6).wait_recv()
        slot = n % LIVE

        def step(k, carry):
            total = part[slot, at(x, z), k].astype(jnp.float32)
            for ref in (land.at[n, 0, z], land.at[n, 1, z], across.at[n]):
                total += ref[k].astype(jnp.float32)
            out[k, n * CHUNK : (n + 1) * CHUNK, :] = total
            return carry

        lax.fori_loop(0, share, step, 0)
        for m in range(7):
            message(n, m).wait_send()

    for n in range(chunks + 3):
        for late, stage in enumerate((begin, second, third, last)):
            if 0 <= n - late < chunks:
                stage(n - late)

    to_near.wait_send()

    @pl.when(odd)
    def _():
        to_far.wait_send()
        pass_on.wait_send()


def correlate(ya, own, windows, groups):
    width = own.shape[1] // 2
    share = BAND // groups
    chunks = width // CHUNK
    fa, fd = segment_tables()
    vmem = pl.BlockSpec(memory_space=pltpu.VMEM)
    block = (share, CHUNK, LAGS)
    return pl.pallas_call(
        pair_kernel,
        out_shape=jax.ShapeDtypeStruct((share, width, LAGS), jnp.float32),
        in_specs=[vmem] * 5,
        out_specs=vmem,
        scratch_shapes=[
            pltpu.VMEM((BINS, width, HELD), jnp.bfloat16),
            pltpu.VMEM((2 * BINS * HELD, width), jnp.float32),
            pltpu.VMEM((2 * BINS * width, width), jnp.float32),
            pltpu.VMEM((OUT_ROWS * CHUNK, LAGS), jnp.float32),
            pltpu.VMEM(own.shape, jnp.bfloat16),
            pltpu.VMEM(own.shape, jnp.bfloat16),
            pltpu.VMEM((LIVE, groups) + block, jnp.bfloat16),
            pltpu.VMEM((chunks, 2) + block, jnp.bfloat16),
            pltpu.VMEM((chunks, 2, 2) + block, jnp.bfloat16),
            pltpu.VMEM((chunks,) + block, jnp.bfloat16),
            pltpu.SemaphoreType.DMA((chunks, 7)),
            pltpu.SemaphoreType.DMA((chunks, 7)),
            pltpu.SemaphoreType.DMA((3,)),
            pltpu.SemaphoreType.DMA((2,)),
        ],
        compiler_params=pltpu.CompilerParams(
            vmem_limit_bytes=62 * 2**20, collective_id=0, has_side_effects=True
        ),
        cost_estimate=pl.CostEstimate(flops=6 * 10**9, bytes_accessed=20 * 10**6, transcendentals=0),
    )(ya, own, jnp.asarray(fa), jnp.asarray(fd), jnp.asarray(lag_table(windows)))


def time_series(record, starts):
    samples = jnp.concatenate(
        [lax.dynamic_slice_in_dim(record, starts[w], SAMP, 0) for w in range(starts.shape[0])], 1
    )
    spec = jnp.dot(jnp.asarray(dft_table()), samples, preferred_element_type=jnp.float32)
    white = whiten(spec).reshape(2 * ROWS, samples.shape[1])
    table = jnp.asarray(inverse_table(SEG * (SLOTS + 2)))
    return jnp.dot(table, white, preferred_element_type=jnp.float32).astype(jnp.bfloat16)


def body(record, starts):
    groups = lax.axis_size("tm")
    ya = time_series(record, starts)
    own = jnp.pad(ya[HALF : HALF + SAMP], ((0, SEG * SLOTS - SAMP), (0, 0)))
    return correlate(ya, own, starts.shape[0] * groups, groups)


def solution(mesh):
    return jax.shard_map(
        body,
        mesh=mesh,
        in_specs=(P("tm", "chan"), P("tm")),
        out_specs=P("tm", "chan", None),
        check_vma=False,
    )
```

time: 437 us -> 157 us (0.36)
  Pallas kernels: 257 us -> 127 us
  waiting for transfers between devices: 130 us -> 0 us
  between operations: 17.4 us -> 3.98 us
  other arithmetic: 6.47 us -> 1.51 us
  starting transfers between devices: 4.95 us -> 0 us
    pallas_call x1, Pallas kernels: 257 us -> 127 us  [correlate(): pl.pallas_call(pair_kernel, out_shape=jax.ShapeDtypeStruct((share, width,...]
    reduce_scatter x1 -> x0, waiting for transfers between devices: 90 us -> none  [body(): total = lax.psum_scatter(part, 'tm', scatter_dimension=0, tiled=True)]
    ppermute x2 -> x0, waiting for transfers between devices: 39.6 us -> none  [the longest x1 35.1 us: body(): after = lax.ppermute(own, 'chan', [(j, j - 1) for j in range(1, blocks)])]
    ppermute x2 -> x0, starting transfers between devices: 4.94 us -> none  [the longest x1 2.57 us: body(): after = lax.ppermute(own, 'chan', [(j, j - 1) for j in range(1, blocks)])]
  transfers between devices with their start and end apart: 3 -> 0, of which waited for: 3 -> 0; matrix products, arithmetic and copies ran while one was open for 0% -> 0% of each run, Pallas kernels for 0% -> 0%
where the time goes in v2:
time: 157 us
  Pallas kernels  127 us (81%)
  matrix products  15.1 us (10%)
  local copies, waits for them, and re-layouts  8.89 us (6%)
  between operations  3.98 us (3%)
    pallas_call x1, Pallas kernels, correlate(): pl.pallas_call(pair_kernel, out_shape=jax.ShapeDtypeStruct((share, width,...  127 us
    dot_general x1, matrix products, time_series(): jnp.dot(jnp.asarray(dft_table()), samples, preferred_element_type=jnp.flo...  9.2 us
    dot_general x1, matrix products, time_series(): jnp.dot(table, white, preferred_element_type=jnp.float32)  5.94 us
    unnamed x13, local copies, waits for them, and re-layouts  4.26 us

profile of v2, /device:TPU:25, one launch (start us, length us, event | category | flops | bytes accessed | tf_op | source)
XLA Modules:
  0.0 156.5 jit_solution(2958096265617753730)
XLA Ops:
  0.0 1.3 fusion.5
  5.2 1.8 %constant_dynamic-slice_fusion.1 = (bf16[3000,128]{1,0:T(8,128)(2,1)S(1)}, bf16[3000,128]{1,0:T(8,128)(2,1)S(1)}) fusion(bf16[8192,128]{1,0:T(8,128)(2,1)} %param.7, s32[]{:T(128)S(6)} %select_n.6, s32[]{:T(128)S(6)} %select_n.7), kind=kLoop, calls=%fused_computation.11 | loop fusion | bytes 3072008 | tf_op jit(solution)/shard_map/dynamic_slice | solution.py:357
  7.0 0.0 slice-start
  7.0 0.0 slice-start.1
  7.0 0.0 slice-start.2
  7.0 0.0 slice-start.3
  7.0 9.2 %fusion.3 = f32[3008,256]{1,0:T(8,128)S(1)} fusion(bf16[3008,3000]{1,0:T(8,128)(2,1)} %constant.25.clone, bf16[3000,128]{1,0:T(8,128)(2,1)S(1)} %get-tuple-element.6, bf16[3000,128]{1,0:T(8,128)(2,1)S(1)} %get-tuple-element.5), kind=kOutput, calls=%fused_computation.9 | convolution fusion | flops 4623360000 | bytes 22664192 | tf_op jit(solution)/shard_map/dot_general | solution.py:359
  16.2 0.0 slice-start.4
  16.2 0.2 fusion.2
  16.4 0.8 maximum_divide_fusion
  17.3 0.5 fusion.1
  17.8 0.0 slice-done
  17.8 0.0 slice-done.1
  17.8 0.0 slice-done.2
  17.8 0.0 slice-done.3
  17.8 1.3 slice-done.4
  19.1 5.9 %fusion.ya = bf16[3200,256]{1,0:T(8,128)(2,1)S(1)} fusion(bf16[3200,3008]{1,0:T(8,128)(2,1)S(1)} %bitcast.12, bf16[3008,256]{1,0:T(8,128)(2,1)S(1)} %fusion.1), kind=kOutput, calls=%fused_computation.1 | convolution fusion | flops 4929126400 | bytes 22429696 | tf_op jit(solution)/shard_map/dot_general | solution.py:362
  25.1 0.0 copy-start
  25.1 0.1 slice.34
  25.2 1.4 pad.9.own
  26.6 0.1 copy-done
  26.8 127.0 %shard_map.73 = f32[25,128,128]{2,1,0:T(8,128)} custom-call(bf16[3200,256]{1,0:T(8,128)(2,1)} %copy-done, bf16[3072,256]{1,0:T(8,128)(2,1)} %pad.9.own, bf16[192,192]{1,0:T(8,128)(2,1)} %constant.27.clone.fa, bf16[192,128]{1,0:T(8,128)(2,1)} %constant.28.clone.fd, bf16[192,128]{1,0:T(8,128)(2,1)} %constant.29.clone.lag), custom_call_target="tpu_custom_call" | custom-call | flops 6000000000 | bytes 20000000 | tf_op jit(solution)/shard_map/pallas_call | solution.py:327
  153.8 2.8 %copy.11 = f32[25,128,128]{2,1,0:T(8,128)} copy(f32[25,128,128]{2,1,0:T(8,128)} %shard_map.73) | data formatting | bytes 3276800
  (1 shorter events, 0.0 us)
Async XLA Ops:
  7.0 10.8 %slice-start = ((s8[19660800]{0:T(1024)(128)(4,1)}), s8[4194304]{0:T(1024)(128)(4,1)S(1)}, s32[]{:S(2)}) async-start(s8[19660800]{0:T(1024)(128)(4,1)} %bitcast.11), calls=%async_computation | async-start | bytes 8388608
  7.0 10.8 %slice-start.1 = ((s8[19660800]{0:T(1024)(128)(4,1)}), s8[4194304]{0:T(1024)(128)(4,1)S(1)}, s32[]{:S(2)}) async-start(s8[19660800]{0:T(1024)(128)(4,1)} %bitcast.11), calls=%async_computation.1 | async-start | bytes 8388608
  7.0 10.8 %slice-start.2 = ((s8[19660800]{0:T(1024)(128)(4,1)}), s8[4194304]{0:T(1024)(128)(4,1)S(1)}, s32[]{:S(2)}) async-start(s8[19660800]{0:T(1024)(128)(4,1)} %bitcast.11), calls=%async_computation.2 | async-start | bytes 8388608
  7.0 10.8 %slice-start.3 = ((s8[19660800]{0:T(1024)(128)(4,1)}), s8[2883584]{0:T(1024)(128)(4,1)S(1)}, s32[]{:S(2)}) async-start(s8[19660800]{0:T(1024)(128)(4,1)} %bitcast.11), calls=%async_computation.3 | async-start | bytes 5767168
  16.2 2.9 %slice-start.4 = ((s8[19660800]{0:T(1024)(128)(4,1)}), s8[4194304]{0:T(1024)(128)(4,1)S(1)}, s32[]{:S(2)}) async-start(s8[19660800]{0:T(1024)(128)(4,1)} %bitcast.11), calls=%async_computation.4 | async-start | bytes 8388608
  25.1 1.7 %copy-start = (bf16[3200,256]{1,0:T(8,128)(2,1)}, bf16[3200,256]{1,0:T(8,128)(2,1)S(1)}, u32[]{:S(2)}) copy-start(bf16[3200,256]{1,0:T(8,128)(2,1)S(1)} %fusion.ya) | copy-start | bytes 4915204

commit v3 on v2

v3 whole, which is shorter than its diff:
```python
import math

import jax
import jax.numpy as jnp
import ml_dtypes
import numpy as np
from jax import lax
from jax.experimental import pallas as pl
from jax.experimental.pallas import tpu as pltpu
from jax.sharding import PartitionSpec as P

SAMP = 3000
F = 1501
ROWS = 1504
BAND = 200
LAGS = 128
HALF = LAGS // 2
SEG = 64
SLOTS = 48
SPAN = 192
POINTS = 191
BINS = 96
BF16 = ml_dtypes.bfloat16


def turns(a, b, period):
    return 2.0 * math.pi * (np.outer(a, b) % period) / period


def dft_table():
    angle = turns(np.arange(F), np.arange(SAMP), SAMP)
    table = np.zeros((2, ROWS, SAMP), np.float32)
    table[0, :F] = np.cos(angle) / math.sqrt(SAMP)
    table[1, :F] = -np.sin(angle) / math.sqrt(SAMP)
    return table.reshape(2 * ROWS, SAMP).astype(BF16)


def inverse_table(rows):
    time = (np.arange(rows) - HALF) % SAMP
    weight = np.full(F, 2.0)
    weight[0] = weight[-1] = 1.0
    angle = turns(time, np.arange(F), SAMP)
    table = np.zeros((rows, 2, ROWS), np.float32)
    table[:, 0, :F] = weight * np.cos(angle) / math.sqrt(SAMP)
    table[:, 1, :F] = -weight * np.sin(angle) / math.sqrt(SAMP)
    return table.reshape(rows, 2 * ROWS).astype(BF16)


def segment_tables():
    angle = turns(np.arange(BINS), np.arange(SPAN), POINTS)
    full = np.stack([np.cos(angle), -np.sin(angle)], axis=1) / math.sqrt(POINTS)
    full = full.reshape(2 * BINS, SPAN)
    full[:, POINTS:] = 0.0
    high = full.astype(BF16)
    low = (full - high.astype(np.float64)).astype(BF16)
    return high, np.concatenate([high[:, :SEG], low[:, :SEG]], axis=1)


def lag_table(windows):
    angle = turns(np.arange(BINS), np.arange(LAGS), POINTS)
    weight = np.full((BINS, 1), 2.0)
    weight[0] = 1.0
    table = np.stack([weight * np.cos(angle), -weight * np.sin(angle)], axis=1)
    return (table / math.sqrt(SAMP * windows)).reshape(2 * BINS, LAGS).astype(BF16)


def whiten(spec):
    parts = spec.reshape(2, ROWS, spec.shape[1])
    power = parts[0] * parts[0] + parts[1] * parts[1]
    padded = jnp.pad(power, ((1, 1), (0, 0)))
    smooth = (padded[:-2] + power + padded[2:]) / 3.0
    factor = 1.0 / jnp.maximum(jnp.sqrt(smooth), 0.5)
    return (parts * factor[None]).astype(jnp.bfloat16)


FIRST = 8
OUT_ROWS = FIRST + BAND + 9
HELD = 2 * 2 * SLOTS
CHUNK = 16
RING = 4
PARTS = 3
BIN_PITCH = 225
NEXT_PITCH = 129
ROW_PITCH = 17
SECOND = 128
NO_FAR = 48
KINDS = "XZXXZXZX"
STEPS = (
    "b0", "b1", "s0", "b2", "f", "s1", "s2", "t0", "t1", "b3", "t2",
    "b4", "b5", "s3", "b6", "s5", "b7", "s4", "t3", "l0", "l1", "t5",
    "l2", "s7", "t4", "s6", "l3", "t7", "l4", "l5", "t6", "l7", "l6",
)
MESH = pl.DeviceIdType.MESH


def unrolled(count, step, times):
    def several(i, carry):
        step([i * times + u for u in range(times)])
        return carry

    lax.fori_loop(0, count // times, several, 0)


def pair_kernel(
    ya, own, fa, fd, lag, out,
    sega, bins, gram, rows, near, far, part, inbox,
    sent, come, sent_y, come_y,
):
    width = own.shape[1] // 2
    share = out.shape[0]
    blocks = lax.axis_size("chan")
    i, j = lax.axis_index("tm"), lax.axis_index("chan")
    x, z = lax.rem(i, RING), i // RING
    right = {"tm": z * RING + lax.rem(x + 1, RING)}
    left = {"tm": z * RING + lax.rem(x + RING - 1, RING)}
    other = {"tm": (1 - z) * RING + x}
    odd = lax.rem(j, 2) == 1

    def behind(distance):
        return {"chan": lax.rem(j + blocks + distance, blocks)}

    barrier = pltpu.get_barrier_semaphore()
    peers = (right, left, other, behind(-1), behind(1), behind(-2), behind(2))
    for device in peers:
        pl.semaphore_signal(barrier, inc=1, device_id=device, device_id_type=MESH)
    pl.semaphore_wait(barrier, len(peers))

    def remote(source, target, send, receive, device):
        return pltpu.make_async_remote_copy(
            src_ref=source, dst_ref=target, send_sem=send, recv_sem=receive,
            device_id=device, device_id_type=MESH,
        )

    length = SLOTS // PARTS * SEG
    to_near = []
    for p in range(PARTS):
        piece = pl.ds(p * length, length)
        to_near.append(
            remote(own.at[piece], near.at[piece], sent_y.at[p], come_y.at[p], behind(-1))
        )
    to_far = remote(own, far, sent_y.at[PARTS], come_y.at[PARTS], behind(-2))
    pass_on = remote(near, far, sent_y.at[PARTS + 1], come_y.at[PARTS], behind(-1))
    for piece in to_near:
        piece.start()

    def spread(slot, s, spec):
        at = slot * SECOND + s
        bins[pl.ds(at, 2 * BINS, stride=BIN_PITCH), :] = spec[:, :width]
        bins[pl.ds(at + SLOTS, 2 * BINS, stride=BIN_PITCH), :] = spec[:, width:]

    def long_segments(index):
        specs = []
        for s in index:
            block = ya[pl.ds(pl.multiple_of(s * SEG, SEG), SPAN), :]
            specs.append(jnp.dot(fa[...], block, preferred_element_type=jnp.float32))
        for s, spec in zip(index, specs):
            spread(0, s, spec)

    def short_segments(source, slot, absent, first, count):
        def step(index):
            specs = []
            for s in index:
                block = source[pl.ds(pl.multiple_of((first + s) * SEG, SEG), SEG), :]
                twice = jnp.concatenate([block, block], 0)
                specs.append(jnp.dot(fd[absent], twice, preferred_element_type=jnp.float32))
            for s, spec in zip(index, specs):
                spread(slot, first + s, spec)

        unrolled(count, step, 8)

    def of_bin(slot, b):
        first = b * 2 * BIN_PITCH + slot * SECOND
        return bins[pl.ds(first, 2 * SLOTS), :], bins[pl.ds(first + BIN_PITCH, 2 * SLOTS), :]

    def turn_bins(index):
        for b in index:
            sega[b] = jnp.concatenate(of_bin(0, b), 0).astype(jnp.bfloat16).T

    def product(slot, b, first):
        real, imag = [part.astype(jnp.bfloat16) for part in of_bin(slot, b)]
        both = jnp.concatenate(
            [jnp.concatenate([real, imag], 0), jnp.concatenate([-imag, real], 0)], 1
        )
        return jnp.dot(sega[b, first:, :], both, preferred_element_type=jnp.float32)

    def keep(target, pitch, b, cross):
        first = b * 2 * pitch
        target[pl.ds(first, width), :] = cross[:, :width]
        target[pl.ds(first + pitch, width), :] = cross[:, width:]

    def gram_next(index):
        for b, cross in zip(index, [product(1, b, 0) for b in index]):
            keep(gram, NEXT_PITCH, b, cross)

    def gram_own(index):
        for b, cross in zip(index, [product(0, b, 0) for b in index]):
            keep(bins, BIN_PITCH, b, cross)

    tall = width - NO_FAR
    same = lax.broadcasted_iota(jnp.int32, (tall, width), 1)
    same = same > lax.broadcasted_iota(jnp.int32, (tall, width), 0) + NO_FAR

    def gram_far(index):
        crosses = [product(1, b, NO_FAR) for b in index]
        places = [pl.ds((2 * b + h) * BIN_PITCH + NO_FAR, tall) for b in index for h in range(2)]
        before = [bins[place, :] for place in places]
        for e, place in enumerate(places):
            h = e % 2
            cross = crosses[e // 2][:, h * width : (h + 1) * width]
            bins[place, :] = jnp.where(same, before[e], cross)

    def place_next(ahead, c):
        return width + ahead - c

    def place_own(ahead, c):
        return jnp.where(ahead + 7 > c, ahead - c, 2 * width + ahead - c)

    def lag_step(source, pitch, place, base):
        def step(index):
            cross = jnp.concatenate(
                [
                    source[pl.ds(base + c, 2 * BINS, stride=pitch), :].astype(jnp.bfloat16)
                    for c in index
                ],
                1,
            )
            lags = lax.dot_general(
                cross, lag[...], (((0,), (0,)), ((), ())), preferred_element_type=jnp.float32
            )
            for u, c in enumerate(index):
                for e in range(width // 8):
                    k = jnp.clip(place(8 * e, base + c), -FIRST, BAND + 1)
                    at = u * width + 8 * e
                    first = (k + FIRST) * ROW_PITCH + c
                    rows[pl.ds(first, 8, stride=ROW_PITCH), :] = lags[at : at + 8]

        return step

    unrolled(SLOTS, long_segments, 8)
    unrolled(BINS, turn_bins, 8)
    short_segments(own, 0, 0, 0, SLOTS)

    @pl.when(odd)
    def _():
        to_far.start()

    unrolled(BINS, gram_own, 8)
    near_absent = jnp.where(j < blocks - 1, 0, 1)
    for p in range(PARTS):
        to_near[p].wait_recv()
        short_segments(near, 1, near_absent, p * (SLOTS // PARTS), SLOTS // PARTS)

    @pl.when(odd)
    def _():
        pass_on.start()

    unrolled(BINS, gram_next, 8)

    def take_far():
        to_far.wait_recv()
        short_segments(far, 1, jnp.where(j < blocks - 2, 0, 1), 0, SLOTS)
        unrolled(BINS, gram_far, 8)

    def at(column, row):
        return row * RING + lax.rem(column + RING, RING)

    half = share // 2 + 1
    low, high, whole = (0, half), (half, share - half), (0, share)

    def message(n, m):
        def block(column, row, ks):
            return part.at[n, at(column, row), pl.ds(*ks)]

        def box(place, ks):
            return inbox.at[n, place, pl.ds(*ks)]

        if KINDS[n] == "X":
            source, target, device = [
                (block(x + 2, 0, whole), box(0, whole), right),
                (block(x + 2, 1, whole), box(1, whole), left),
                (block(x + 1, 1, whole), box(3, whole), right),
                (block(x - 1, 0, whole), box(4, whole), left),
                (block(x + 1, 0, whole), box(2, whole), right),
                (block(x - 1, 1, whole), box(5, whole), left),
                (block(x, 1 - z, whole), box(6, whole), other),
            ][m]
        else:
            source, target, device = [
                (part.at[n, pl.ds((1 - z) * RING, RING)], inbox.at[n, pl.ds(0, RING)], other),
                (block(x + 2, z, low), box(4, low), right),
                (block(x + 2, z, high), box(4, high), left),
                (block(x + 1, z, high), box(5, high), right),
                (block(x - 1, z, low), box(6, low), left),
                (block(x + 1, z, low), box(5, low), right),
                (block(x - 1, z, high), box(6, high), left),
            ][m]
        return remote(source, target, sent.at[n, m], come.at[n, m], device)

    def start(n, *which):
        for m in which:
            message(n, m).start()

    def wait(n, *which):
        for m in which:
            message(n, m).wait_recv()

    def plus(n, place, boxes, ks):
        first, count = ks

        def step(index):
            for k in index:
                total = part[n, place, first + k].astype(jnp.float32)
                for box in boxes:
                    total += inbox[n, box, first + k].astype(jnp.float32)
                part[n, place, first + k] = total.astype(jnp.bfloat16)

        unrolled(count, step, 5 if count % 5 == 0 else count)

    def begin(n):
        unrolled(CHUNK, lag_step(gram, NEXT_PITCH, place_next, n * CHUNK), 8)
        unrolled(CHUNK, lag_step(bins, BIN_PITCH, place_own, n * CHUNK), 8)

        def step(index):
            for k in index:
                for d in range(BAND // share):
                    first = (d * share + k + FIRST + 1) * ROW_PITCH
                    part[n, d, k] = rows[pl.ds(first, CHUNK), :].astype(jnp.bfloat16)

        unrolled(share, step, 5)
        start(n, *((0, 1, 2, 3) if KINDS[n] == "X" else (0,)))

    def second(n):
        if KINDS[n] == "X":
            wait(n, 0, 1)
            plus(n, at(x + 1, 0), [0], whole)
            start(n, 4)
            plus(n, at(x - 1, 1), [1], whole)
            start(n, 5)
        else:
            wait(n, 0)
            for step in (2, 1, 3, 0):
                plus(n, at(x + step, z), [(x + step) % RING], whole)
                start(n, *{2: (1, 2), 1: (3,), 3: (4,), 0: ()}[step])

    def third(n):
        if KINDS[n] == "X":
            wait(n, 2, 3, 4, 5)
            plus(n, at(x, 1 - z), [3 - z, 5 - z], whole)
            start(n, 6)
        else:
            wait(n, 1, 2)
            plus(n, at(x + 1, z), [4], low)
            start(n, 5)
            plus(n, at(x - 1, z), [4], high)
            start(n, 6)

    def last(n):
        if KINDS[n] == "X":
            wait(n, 6)
            boxes = (2 + z, 4 + z, 6)
        else:
            wait(n, 3, 4, 5, 6)
            boxes = (5, 6)

        def step(index):
            for k in index:
                total = part[n, at(x, z), k].astype(jnp.float32)
                for box in boxes:
                    total += inbox[n, box, k].astype(jnp.float32)
                out[k, n * CHUNK : (n + 1) * CHUNK, :] = total

        unrolled(share, step, 5)
        for m in range(7):
            message(n, m).wait_send()

    stages = {"b": begin, "s": second, "t": third, "l": last}
    for name in STEPS:
        if name == "f":
            take_far()
        else:
            stages[name[0]](int(name[1:]))

    for piece in to_near:
        piece.wait_send()

    @pl.when(odd)
    def _():
        to_far.wait_send()
        pass_on.wait_send()


def correlate(ya, own, windows, groups):
    width = own.shape[1] // 2
    share = BAND // groups
    chunks = width // CHUNK
    fa, fd = segment_tables()
    fd = np.stack([fd, np.zeros_like(fd)])
    vmem = pl.BlockSpec(memory_space=pltpu.VMEM)
    block = (share, CHUNK, LAGS)
    return pl.pallas_call(
        pair_kernel,
        out_shape=jax.ShapeDtypeStruct((share, width, LAGS), jnp.float32),
        in_specs=[vmem] * 5,
        out_specs=vmem,
        scratch_shapes=[
            pltpu.VMEM((BINS, width, HELD), jnp.bfloat16),
            pltpu.VMEM((2 * BINS * BIN_PITCH, width), jnp.float32),
            pltpu.VMEM((2 * BINS * NEXT_PITCH, width), jnp.float32),
            pltpu.VMEM((OUT_ROWS * ROW_PITCH, LAGS), jnp.float32),
            pltpu.VMEM(own.shape, jnp.bfloat16),
            pltpu.VMEM(own.shape, jnp.bfloat16),
            pltpu.VMEM((chunks, groups) + block, jnp.bfloat16),
            pltpu.VMEM((chunks, 7) + block, jnp.bfloat16),
            pltpu.SemaphoreType.DMA((chunks, 7)),
            pltpu.SemaphoreType.DMA((chunks, 7)),
            pltpu.SemaphoreType.DMA((PARTS + 2,)),
            pltpu.SemaphoreType.DMA((PARTS + 1,)),
        ],
        compiler_params=pltpu.CompilerParams(
            vmem_limit_bytes=62 * 2**20, collective_id=0, has_side_effects=True
        ),
        cost_estimate=pl.CostEstimate(flops=6 * 10**9, bytes_accessed=20 * 10**6, transcendentals=0),
    )(ya, own, jnp.asarray(fa), jnp.asarray(fd), jnp.asarray(lag_table(windows)))


def time_series(record, starts):
    samples = jnp.concatenate(
        [lax.dynamic_slice_in_dim(record, starts[w], SAMP, 0) for w in range(starts.shape[0])], 1
    )
    spec = jnp.dot(jnp.asarray(dft_table()), samples, preferred_element_type=jnp.float32)
    white = whiten(spec).reshape(2 * ROWS, samples.shape[1])
    table = jnp.asarray(inverse_table(SEG * (SLOTS + 2)))
    return jnp.dot(table, white, preferred_element_type=jnp.float32).astype(jnp.bfloat16)


def body(record, starts):
    groups = lax.axis_size("tm")
    ya = time_series(record, starts)
    own = jnp.pad(ya[HALF : HALF + SAMP], ((0, SEG * SLOTS - SAMP), (0, 0)))
    return correlate(ya, own, starts.shape[0] * groups, groups)


def solution(mesh):
    return jax.shard_map(
        body,
        mesh=mesh,
        in_specs=(P("tm", "chan"), P("tm")),
        out_specs=P("tm", "chan", None),
        check_vma=False,
    )
```

time: 157 us -> 122 us (0.78)
  Pallas kernels: 127 us -> 91.8 us
    pallas_call x1, Pallas kernels: 127 us -> 91.8 us  [correlate(): pl.pallas_call(pair_kernel, out_shape=jax.ShapeDtypeStruct((share, width,...]
where the time goes in v3:
time: 122 us; the launch traced here: 121 us
  Pallas kernels  91.8 us (75%)
  matrix products  15.1 us (12%)
  local copies, waits for them, and re-layouts  8.89 us (7%)
  between operations  3.98 us (3%)
  other arithmetic  1.51 us (1%)
    pallas_call x1, Pallas kernels, correlate(): pl.pallas_call(pair_kernel, out_shape=jax.ShapeDtypeStruct((share, width,...  91.8 us
    dot_general x1, matrix products, time_series(): jnp.dot(jnp.asarray(dft_table()), samples, preferred_element_type=jnp.flo...  9.2 us
    dot_general x1, matrix products, time_series(): jnp.dot(table, white, preferred_element_type=jnp.float32)  5.94 us
    unnamed x13, local copies, waits for them, and re-layouts  4.26 us

profile of v3, /device:TPU:25, one launch (start us, length us, event | category | flops | bytes accessed | tf_op | source)
XLA Modules:
  0.0 121.3 jit_solution(3212181984098269413)
XLA Ops:
  0.0 1.3 %fusion.5 = (s32[1]{0:T(128)}, s32[1]{0:T(128)}) fusion(s32[2]{0:T(128)} %param.8), kind=kLoop, calls=%fused_computation.13 | loop fusion | bytes 16 | tf_op jit(solution)/shard_map/slice | solution.py:428
  5.2 1.8 %constant_dynamic-slice_fusion.1 = (bf16[3000,128]{1,0:T(8,128)(2,1)S(1)}, bf16[3000,128]{1,0:T(8,128)(2,1)S(1)}) fusion(bf16[8192,128]{1,0:T(8,128)(2,1)} %param.7, s32[]{:T(128)S(6)} %select_n.6, s32[]{:T(128)S(6)} %select_n.7), kind=kLoop, calls=%fused_computation.11 | loop fusion | bytes 3072008 | tf_op jit(solution)/shard_map/dynamic_slice | solution.py:428
  7.0 0.0 slice-start
  7.0 0.0 slice-start.1
  7.0 0.0 slice-start.2
  7.0 0.0 slice-start.3
  7.0 9.2 %fusion.3 = f32[3008,256]{1,0:T(8,128)S(1)} fusion(bf16[3008,3000]{1,0:T(8,128)(2,1)} %constant.25.clone, bf16[3000,128]{1,0:T(8,128)(2,1)S(1)} %get-tuple-element.6, bf16[3000,128]{1,0:T(8,128)(2,1)S(1)} %get-tuple-element.5), kind=kOutput, calls=%fused_computation.9 | convolution fusion | flops 4623360000 | bytes 22664192 | tf_op jit(solution)/shard_map/dot_general | solution.py:430
  16.2 0.0 slice-start.4
  16.2 0.2 fusion.2
  16.4 0.8 maximum_divide_fusion
  17.3 0.5 fusion.1
  17.8 0.0 slice-done
  17.8 0.0 slice-done.1
  17.8 0.0 slice-done.2
  17.8 0.0 slice-done.3
  17.8 1.3 %slice-done.4 = s8[4194304]{0:T(1024)(128)(4,1)S(1)} async-done(((s8[19660800]{0:T(1024)(128)(4,1)}), s8[4194304]{0:T(1024)(128)(4,1)S(1)}, s32[]{:S(2)}) %slice-start.4) | async-done | bytes 4194328
  19.1 5.9 %fusion.ya = bf16[3200,256]{1,0:T(8,128)(2,1)S(1)} fusion(bf16[3200,3008]{1,0:T(8,128)(2,1)S(1)} %bitcast.12, bf16[3008,256]{1,0:T(8,128)(2,1)S(1)} %fusion.1), kind=kOutput, calls=%fused_computation.1 | convolution fusion | flops 4929126400 | bytes 22429696 | tf_op jit(solution)/shard_map/dot_general | solution.py:433
  25.1 0.0 copy-start
  25.1 0.1 slice.34
  25.2 1.4 %pad.9.own = bf16[3072,256]{1,0:T(8,128)(2,1)} pad(bf16[3000,256]{1,0:T(8,128)(2,1)S(1)} %slice.34, bf16[]{:T(256)} %constant.24.clone.1), padding=0_72x0_0 | pad | bytes 3108866 | tf_op jit(solution)/shard_map/jit(_pad)/pad | solution.py:439
  26.6 0.1 copy-done
  26.8 91.8 %shard_map.73 = f32[25,128,128]{2,1,0:T(8,128)} custom-call(bf16[3200,256]{1,0:T(8,128)(2,1)} %copy-done, bf16[3072,256]{1,0:T(8,128)(2,1)} %pad.9.own, bf16[192,192]{1,0:T(8,128)(2,1)} %constant.27.clone.fa, bf16[2,192,128]{2,1,0:T(8,128)(2,1)} %constant.28.clone.fd, bf16[192,128]{1,0:T(8,128)(2,1)} %constant.29.clone.lag), custom_call_target="tpu_custom_call" | custom-call | flops 6000000000 | bytes 20000000 | tf_op jit(solution)/shard_map/pallas_call | solution.py:400
  118.5 2.8 %copy.11 = f32[25,128,128]{2,1,0:T(8,128)} copy(f32[25,128,128]{2,1,0:T(8,128)} %shard_map.73) | data formatting | bytes 3276800
  (1 shorter events, 0.0 us)
Async XLA Ops:
  7.0 10.8 %slice-start = ((s8[19660800]{0:T(1024)(128)(4,1)}), s8[4194304]{0:T(1024)(128)(4,1)S(1)}, s32[]{:S(2)}) async-start(s8[19660800]{0:T(1024)(128)(4,1)} %bitcast.11), calls=%async_computation | async-start | bytes 8388608
  7.0 10.8 %slice-start.1 = ((s8[19660800]{0:T(1024)(128)(4,1)}), s8[4194304]{0:T(1024)(128)(4,1)S(1)}, s32[]{:S(2)}) async-start(s8[19660800]{0:T(1024)(128)(4,1)} %bitcast.11), calls=%async_computation.1 | async-start | bytes 8388608
  7.0 10.8 %slice-start.2 = ((s8[19660800]{0:T(1024)(128)(4,1)}), s8[4194304]{0:T(1024)(128)(4,1)S(1)}, s32[]{:S(2)}) async-start(s8[19660800]{0:T(1024)(128)(4,1)} %bitcast.11), calls=%async_computation.2 | async-start | bytes 8388608
  7.0 10.8 %slice-start.3 = ((s8[19660800]{0:T(1024)(128)(4,1)}), s8[2883584]{0:T(1024)(128)(4,1)S(1)}, s32[]{:S(2)}) async-start(s8[19660800]{0:T(1024)(128)(4,1)} %bitcast.11), calls=%async_computation.3 | async-start | bytes 5767168
  16.2 2.9 %slice-start.4 = ((s8[19660800]{0:T(1024)(128)(4,1)}), s8[4194304]{0:T(1024)(128)(4,1)S(1)}, s32[]{:S(2)}) async-start(s8[19660800]{0:T(1024)(128)(4,1)} %bitcast.11), calls=%async_computation.4 | async-start | bytes 8388608
  25.1 1.7 %copy-start = (bf16[3200,256]{1,0:T(8,128)(2,1)}, bf16[3200,256]{1,0:T(8,128)(2,1)S(1)}, u32[]{:S(2)}) copy-start(bf16[3200,256]{1,0:T(8,128)(2,1)S(1)} %fusion.ya) | copy-start | bytes 4915204

commit v4 on v3

--- a/solution.py
+++ b/solution.py
@@ -11,15 +11,19 @@
 
 SAMP = 3000
 F = 1501
-ROWS = 1504
+PAD = 3072
+PIECE = 192
+PIECES = 8
 BAND = 200
 LAGS = 128
 HALF = LAGS // 2
 SEG = 64
 SLOTS = 48
+FULL = SAMP // SEG
 SPAN = 192
 POINTS = 191
 BINS = 96
+SERIES = SEG * (SLOTS + 2)
 BF16 = ml_dtypes.bfloat16
 
 
@@ -27,23 +31,27 @@
     return 2.0 * math.pi * (np.outer(a, b) % period) / period
 
 
+def by_pieces(real, imag):
+    parts = np.zeros((2, PIECES * PIECE) + real.shape[1:], np.float32)
+    parts[0, :F], parts[1, :F] = real, imag
+    parts = parts.reshape((2, PIECES, PIECE) + real.shape[1:])
+    return np.moveaxis(parts, 0, 1).reshape((PAD,) + real.shape[1:])
+
+
 def dft_table():
     angle = turns(np.arange(F), np.arange(SAMP), SAMP)
-    table = np.zeros((2, ROWS, SAMP), np.float32)
-    table[0, :F] = np.cos(angle) / math.sqrt(SAMP)
-    table[1, :F] = -np.sin(angle) / math.sqrt(SAMP)
-    return table.reshape(2 * ROWS, SAMP).astype(BF16)
-
-
-def inverse_table(rows):
-    time = (np.arange(rows) - HALF) % SAMP
-    weight = np.full(F, 2.0)
+    table = by_pieces(np.cos(angle), -np.sin(angle)) / math.sqrt(SAMP)
+    return np.pad(table, ((0, 0), (0, PAD - SAMP))).astype(BF16)
+
+
+def inverse_table():
+    time = (np.arange(SERIES) - HALF) % SAMP
+    weight = np.full((F, 1), 2.0)
     weight[0] = weight[-1] = 1.0
-    angle = turns(time, np.arange(F), SAMP)
-    table = np.zeros((rows, 2, ROWS), np.float32)
-    table[:, 0, :F] = weight * np.cos(angle) / math.sqrt(SAMP)
-    table[:, 1, :F] = -weight * np.sin(angle) / math.sqrt(SAMP)
-    return table.reshape(rows, 2 * ROWS).astype(BF16)
+    angle = turns(np.arange(F), time, SAMP)
+    table = by_pieces(weight * np.cos(angle), -weight * np.sin(angle)).T / math.sqrt(SAMP)
+    table = table.reshape(PIECES, SERIES // PIECES, PAD // 128, 128)
+    return np.moveaxis(table, 2, 1).reshape(-1, 128).astype(BF16)
 
 
 def segment_tables():
@@ -53,7 +61,10 @@
     full[:, POINTS:] = 0.0
     high = full.astype(BF16)
     low = (full - high.astype(np.float64)).astype(BF16)
-    return high, np.concatenate([high[:, :SEG], low[:, :SEG]], axis=1)
+    short = np.stack([high[:, :SEG], low[:, :SEG]])
+    short = np.stack([short, np.zeros_like(short), short])
+    short[2, :, :, SAMP % SEG :] = 0.0
+    return high, np.concatenate([short[:, 0], short[:, 1]], axis=2)
 
 
 def lag_table(windows):
@@ -64,25 +75,100 @@
     return (table / math.sqrt(SAMP * windows)).reshape(2 * BINS, LAGS).astype(BF16)
 
 
-def whiten(spec):
-    parts = spec.reshape(2, ROWS, spec.shape[1])
-    power = parts[0] * parts[0] + parts[1] * parts[1]
-    padded = jnp.pad(power, ((1, 1), (0, 0)))
-    smooth = (padded[:-2] + power + padded[2:]) / 3.0
-    factor = 1.0 / jnp.maximum(jnp.sqrt(smooth), 0.5)
-    return (parts * factor[None]).astype(jnp.bfloat16)
+TALL = 3024
+EDGE = 8
+
+
+def white_kernel(starts, record, table, white, held, raw, wide, samples, spec, power, sems, wins):
+    width = record.shape[1]
+    rows = 2 * PIECE
+    loads = []
+    for w in range(2):
+        base = jnp.minimum(starts[w] // 16 * 16, record.shape[0] - TALL)
+        base = pl.multiple_of(base, 16)
+        loads.append(
+            pltpu.make_async_copy(record.at[pl.ds(base, TALL)], raw.at[w], wins.at[w])
+        )
+        loads[w].start()
+    pieces = [
+        pltpu.make_async_copy(
+            table.at[pl.ds(i * rows, rows)], held.at[pl.ds(i * rows, rows)], sems.at[i]
+        )
+        for i in range(PIECES)
+    ]
+    for piece in pieces:
+        piece.start()
+    power[:EDGE, :] = jnp.zeros((EDGE, 2 * width), jnp.float32)
+    power[EDGE + PIECES * PIECE :, :] = jnp.zeros((EDGE, 2 * width), jnp.float32)
+    for w in range(2):
+        shift = starts[w] - jnp.minimum(starts[w] // 16 * 16, record.shape[0] - TALL)
+        loads[w].wait()
+        wide[w, :TALL, :] = raw[w].astype(jnp.float32)
+        wide[w, TALL:, :] = jnp.zeros((wide.shape[1] - TALL, width), jnp.float32)
+        samples[:, w * width : (w + 1) * width] = wide[w, pl.ds(shift, PAD), :].astype(jnp.bfloat16)
+
+    def finish(i):
+        at = EDGE + i * PIECE
+        near = [power[at + d : at + d + PIECE, :] for d in (-1, 0, 1)]
+        smooth = (near[0] + near[1] + near[2]) / 3.0
+        factor = 1.0 / jnp.maximum(jnp.sqrt(smooth), 0.5)
+        for h in range(2):
+            part = slice(i * rows + h * PIECE, i * rows + (h + 1) * PIECE)
+            white[part, :] = (spec[part, :] * factor).astype(jnp.bfloat16)
+
+    for i in range(PIECES):
+        pieces[i].wait()
+        part = slice(i * rows, (i + 1) * rows)
+        found = jnp.dot(held[part, :], samples[...], preferred_element_type=jnp.float32)
+        spec[part, :] = found
+        real, imag = found[:PIECE], found[PIECE:]
+        power[EDGE + i * PIECE : EDGE + (i + 1) * PIECE, :] = real * real + imag * imag
+        if i:
+            finish(i - 1)
+    finish(PIECES - 1)
+
+
+def whitened(record, starts):
+    width = record.shape[1]
+    return pl.pallas_call(
+        white_kernel,
+        out_shape=jax.ShapeDtypeStruct((PAD, 2 * width), jnp.bfloat16),
+        in_specs=[
+            pl.BlockSpec(memory_space=pltpu.SMEM),
+            pl.BlockSpec(memory_space=pl.ANY),
+            pl.BlockSpec(memory_space=pl.ANY),
+        ],
+        out_specs=pl.BlockSpec(memory_space=pltpu.VMEM),
+        scratch_shapes=[
+            pltpu.VMEM((PAD, PAD), jnp.bfloat16),
+            pltpu.VMEM((2, TALL, width), jnp.bfloat16),
+            pltpu.VMEM((2, PAD + 32, width), jnp.float32),
+            pltpu.VMEM((PAD, 2 * width), jnp.bfloat16),
+            pltpu.VMEM((PAD, 2 * width), jnp.float32),
+            pltpu.VMEM((PIECES * PIECE + 2 * EDGE, 2 * width), jnp.float32),
+            pltpu.SemaphoreType.DMA((PIECES,)),
+            pltpu.SemaphoreType.DMA((2,)),
+        ],
+        compiler_params=pltpu.CompilerParams(vmem_limit_bytes=62 * 2**20),
+        cost_estimate=pl.CostEstimate(
+            flops=5 * 10**9, bytes_accessed=22 * 10**6, transcendentals=400_000
+        ),
+    )(starts, record, jnp.asarray(dft_table()))
 
 
 FIRST = 8
 OUT_ROWS = FIRST + BAND + 9
 HELD = 2 * 2 * SLOTS
 CHUNK = 16
+BOXES = 7
 RING = 4
-PARTS = 3
+PARTS = 6
 BIN_PITCH = 225
 NEXT_PITCH = 129
 ROW_PITCH = 17
 SECOND = 128
+EXTRA = 8
+EXTRA_ROWS = 384
 NO_FAR = 48
 KINDS = "XZXXZXZX"
 STEPS = (
@@ -102,11 +188,11 @@
 
 
 def pair_kernel(
-    ya, own, fa, fd, lag, out,
-    sega, bins, gram, rows, near, far, part, inbox,
-    sent, come, sent_y, come_y,
+    white, inverse, fa, fd, lag, out,
+    sega, bins, gram, rows, ya, near, pack, extra, far, part, inbox, stage,
+    sent, come, sent_y, come_y, local,
 ):
-    width = own.shape[1] // 2
+    width = out.shape[1]
     share = out.shape[0]
     blocks = lax.axis_size("chan")
     i, j = lax.axis_index("tm"), lax.axis_index("chan")
@@ -119,6 +205,17 @@
     def behind(distance):
         return {"chan": lax.rem(j + blocks + distance, blocks)}
 
+    piece = SERIES // PIECES
+    area = piece * (PAD // 128)
+    tables = [
+        pltpu.make_async_copy(
+            inverse.at[pl.ds(c * area, area)], part.at[pl.ds(c % 2 * area, area)], local.at[c % 2]
+        )
+        for c in range(PIECES)
+    ]
+    tables[0].start()
+    tables[1].start()
+
     barrier = pltpu.get_barrier_semaphore()
     peers = (right, left, other, behind(-1), behind(1), behind(-2), behind(2))
     for device in peers:
@@ -132,16 +229,85 @@
         )
 
     length = SLOTS // PARTS * SEG
-    to_near = []
-    for p in range(PARTS):
-        piece = pl.ds(p * length, length)
-        to_near.append(
-            remote(own.at[piece], near.at[piece], sent_y.at[p], come_y.at[p], behind(-1))
-        )
-    to_far = remote(own, far, sent_y.at[PARTS], come_y.at[PARTS], behind(-2))
-    pass_on = remote(near, far, sent_y.at[PARTS + 1], come_y.at[PARTS], behind(-1))
-    for piece in to_near:
-        piece.start()
+    to_near = [
+        remote(
+            ya.at[pl.ds(SEG + p * length, length)], near.at[pl.ds(p * length, length)],
+            sent_y.at[p], come_y.at[p], behind(-1),
+        )
+        for p in range(PARTS)
+    ]
+    to_far = [
+        remote(pack, far.at[0], sent_y.at[PARTS], come_y.at[PARTS], behind(-2)),
+        remote(
+            extra, far.at[1, pl.ds(0, EXTRA_ROWS)],
+            sent_y.at[PARTS + 1], come_y.at[PARTS + 1], behind(-2),
+        ),
+    ]
+    pass_on = [
+        remote(
+            near.at[:, pl.ds(w * width, width)], far.at[w],
+            sent_y.at[PARTS + 2 + w], come_y.at[PARTS + w], behind(-1),
+        )
+        for w in range(2)
+    ]
+
+    lane = lax.broadcasted_iota(jnp.int32, (SEG, width), 1)
+    begun = 0
+    for c in range(PIECES):
+        tables[c].wait()
+        total = jnp.zeros((piece, 2 * width), jnp.float32)
+        for p in range(0, PAD // 128, 2):
+            first = c % 2 * area + p * piece
+            block = jnp.concatenate(
+                [part[first : first + piece, :], part[first + piece : first + 2 * piece, :]], 1
+            )
+            total += jnp.dot(
+                block, white[p * 128 : (p + 2) * 128, :], preferred_element_type=jnp.float32
+            )
+        ya[c * piece : (c + 1) * piece, :] = total.astype(jnp.bfloat16)
+        if c + 2 < PIECES:
+            tables[c + 2].start()
+        while begun < PARTS and SEG + (begun + 1) * length <= (c + 1) * piece:
+            to_near[begun].start()
+            begun += 1
+
+    def pack_segments(index):
+        for s in index:
+            block = ya[pl.ds(pl.multiple_of((s + 1) * SEG, SEG), SEG), :].astype(jnp.float32)
+            turned = pltpu.roll(block[:, width:], width // 2, 1)
+            pack[pl.ds(pl.multiple_of(s * SEG, SEG), SEG), :] = jnp.where(
+                lane < width // 2, block[:, :width], turned
+            ).astype(jnp.bfloat16)
+
+    def pack_extra(index):
+        for e in index:
+            total = jnp.zeros((SEG, width), jnp.float32)
+            for g in range(PAD // EXTRA_ROWS):
+                first = pl.multiple_of((e + 1) * SEG, SEG) + g * EXTRA_ROWS
+                block = ya[pl.ds(first, SEG), :].astype(jnp.float32)
+                for w in range(2):
+                    place = (2 * g + w) * EXTRA
+                    turned = pltpu.roll(
+                        block[:, w * width : (w + 1) * width], (place + width // 2) % width, 1
+                    )
+                    total = jnp.where((lane >= place) & (lane < place + EXTRA), turned, total)
+            extra[pl.ds(pl.multiple_of(e * SEG, SEG), SEG), :] = total.astype(jnp.bfloat16)
+
+    def far_block(s):
+        group, row = s // (EXTRA_ROWS // SEG), lax.rem(s, EXTRA_ROWS // SEG)
+        first = far[0, pl.ds(pl.multiple_of(s * SEG, SEG), SEG), :].astype(jnp.float32)
+        row = jnp.where(odd, row, s)
+        rest = far[1, pl.ds(pl.multiple_of(row * SEG, SEG), SEG), :].astype(jnp.float32)
+        half = width // 2
+        both = []
+        for w in range(2):
+            body = first if w == 0 else pltpu.roll(first, half, 1)
+            turn = lax.rem(half + width - (2 * group + w) * EXTRA, width)
+            both.append(jnp.where(lane < half, body, pltpu.roll(rest, turn, 1)))
+        block = jnp.concatenate(
+            [jnp.where(odd, both[0], first), jnp.where(odd, both[1], rest)], 1
+        )
+        return block.astype(jnp.bfloat16)
 
     def spread(slot, s, spec):
         at = slot * SECOND + s
@@ -156,17 +322,26 @@
         for s, spec in zip(index, specs):
             spread(0, s, spec)
 
-    def short_segments(source, slot, absent, first, count):
+    def short_segments(block_of, slot, absent, first, count):
         def step(index):
             specs = []
             for s in index:
-                block = source[pl.ds(pl.multiple_of((first + s) * SEG, SEG), SEG), :]
+                s = first + s
+                block = block_of(s)
                 twice = jnp.concatenate([block, block], 0)
-                specs.append(jnp.dot(fd[absent], twice, preferred_element_type=jnp.float32))
+                kind = jnp.where(s < FULL, 0, jnp.where(s == FULL, 2, 1))
+                kind = jnp.where(absent, 1, kind)
+                specs.append(jnp.dot(fd[kind], twice, preferred_element_type=jnp.float32))
             for s, spec in zip(index, specs):
                 spread(slot, first + s, spec)
 
         unrolled(count, step, 8)
+
+    def own_block(s):
+        return ya[pl.ds(pl.multiple_of((s + 1) * SEG, SEG), SEG), :]
+
+    def near_block(s):
+        return near[pl.ds(pl.multiple_of(s * SEG, SEG), SEG), :]
 
     def of_bin(slot, b):
         first = b * 2 * BIN_PITCH + slot * SECOND
@@ -238,27 +413,33 @@
 
     unrolled(SLOTS, long_segments, 8)
     unrolled(BINS, turn_bins, 8)
-    short_segments(own, 0, 0, 0, SLOTS)
+    short_segments(own_block, 0, False, 0, SLOTS)
+    unrolled(BINS, gram_own, 8)
+    unrolled(SLOTS, pack_segments, 8)
+    unrolled(EXTRA_ROWS // SEG, pack_extra, 1)
+    for p in range(PARTS):
+        to_near[p].wait_recv()
+        short_segments(near_block, 1, j == blocks - 1, p * (SLOTS // PARTS), SLOTS // PARTS)
 
     @pl.when(odd)
     def _():
-        to_far.start()
-
-    unrolled(BINS, gram_own, 8)
-    near_absent = jnp.where(j < blocks - 1, 0, 1)
-    for p in range(PARTS):
-        to_near[p].wait_recv()
-        short_segments(near, 1, near_absent, p * (SLOTS // PARTS), SLOTS // PARTS)
-
-    @pl.when(odd)
-    def _():
-        pass_on.start()
+        for copy in to_far + pass_on:
+            copy.start()
 
     unrolled(BINS, gram_next, 8)
 
     def take_far():
-        to_far.wait_recv()
-        short_segments(far, 1, jnp.where(j < blocks - 2, 0, 1), 0, SLOTS)
+        @pl.when(odd)
+        def _():
+            for copy in to_far:
+                copy.wait_recv()
+
+        @pl.when(jnp.logical_not(odd))
+        def _():
+            for copy in pass_on:
+                copy.wait_recv()
+
+        short_segments(far_block, 1, j >= blocks - 2, 0, SLOTS)
         unrolled(BINS, gram_far, 8)
 
     def at(column, row):
@@ -267,12 +448,21 @@
     half = share // 2 + 1
     low, high, whole = (0, half), (half, share - half), (0, share)
 
+    def spot(n, place, k, per):
+        return pl.multiple_of(((n * per + place) * share + k) * CHUNK, CHUNK)
+
+    def part_at(n, place, k=0, count=1):
+        return pl.ds(spot(n, place, k, BAND // share), count * CHUNK)
+
+    def inbox_at(n, place, k=0, count=1):
+        return pl.ds(spot(n, place, k, BOXES), count * CHUNK)
+
     def message(n, m):
         def block(column, row, ks):
-            return part.at[n, at(column, row), pl.ds(*ks)]
+            return part.at[part_at(n, at(column, row), *ks)]
 
         def box(place, ks):
-            return inbox.at[n, place, pl.ds(*ks)]
+            return inbox.at[inbox_at(n, place, *ks)]
 
         if KINDS[n] == "X":
             source, target, device = [
@@ -285,8 +475,9 @@
                 (block(x, 1 - z, whole), box(6, whole), other),
             ][m]
         else:
+            four = (0, RING * share)
             source, target, device = [
-                (part.at[n, pl.ds((1 - z) * RING, RING)], inbox.at[n, pl.ds(0, RING)], other),
+                (part.at[part_at(n, (1 - z) * RING, *four)], box(0, four), other),
                 (block(x + 2, z, low), box(4, low), right),
                 (block(x + 2, z, high), box(4, high), left),
                 (block(x + 1, z, high), box(5, high), right),
@@ -304,15 +495,19 @@
         for m in which:
             message(n, m).wait_recv()
 
+    def summed(n, place, boxes, k):
+        total = part[part_at(n, place, k), :].astype(jnp.float32)
+        for box in boxes:
+            total += inbox[inbox_at(n, box, k), :].astype(jnp.float32)
+        return total
+
     def plus(n, place, boxes, ks):
         first, count = ks
 
         def step(index):
             for k in index:
-                total = part[n, place, first + k].astype(jnp.float32)
-                for box in boxes:
-                    total += inbox[n, box, first + k].astype(jnp.float32)
-                part[n, place, first + k] = total.astype(jnp.bfloat16)
+                total = summed(n, place, boxes, first + k)
+                part[part_at(n, place, first + k), :] = total.astype(jnp.bfloat16)
 
         unrolled(count, step, 5 if count % 5 == 0 else count)
 
@@ -324,7 +519,7 @@
             for k in index:
                 for d in range(BAND // share):
                     first = (d * share + k + FIRST + 1) * ROW_PITCH
-                    part[n, d, k] = rows[pl.ds(first, CHUNK), :].astype(jnp.bfloat16)
+                    part[part_at(n, d, k), :] = rows[pl.ds(first, CHUNK), :].astype(jnp.bfloat16)
 
         unrolled(share, step, 5)
         start(n, *((0, 1, 2, 3) if KINDS[n] == "X" else (0,)))
@@ -362,17 +557,30 @@
             wait(n, 3, 4, 5, 6)
             boxes = (5, 6)
 
+        slot = n % 2
+        if n in shown:
+            shown[n].wait()
+
         def step(index):
             for k in index:
-                total = part[n, at(x, z), k].astype(jnp.float32)
-                for box in boxes:
-                    total += inbox[n, box, k].astype(jnp.float32)
-                out[k, n * CHUNK : (n + 1) * CHUNK, :] = total
+                stage[slot, k] = summed(n, at(x, z), boxes, k)
 
         unrolled(share, step, 5)
+        result(n).start()
         for m in range(7):
             message(n, m).wait_send()
 
+    def result(n):
+        return pltpu.make_async_copy(
+            stage.at[n % 2], out.at[:, pl.ds(n * CHUNK, CHUNK)], local.at[2 + n % 2]
+        )
+
+    order = [int(name[1:]) for name in STEPS if name[0] == "l"]
+    shown, ending = {}, {}
+    for n in order:
+        if n % 2 in ending:
+            shown[n] = result(ending[n % 2])
+        ending[n % 2] = n
     stages = {"b": begin, "s": second, "t": third, "l": last}
     for name in STEPS:
         if name == "f":
@@ -380,64 +588,66 @@
         else:
             stages[name[0]](int(name[1:]))
 
-    for piece in to_near:
-        piece.wait_send()
+    for n in ending.values():
+        result(n).wait()
+    for copy in to_near:
+        copy.wait_send()
 
     @pl.when(odd)
     def _():
-        to_far.wait_send()
-        pass_on.wait_send()
-
-
-def correlate(ya, own, windows, groups):
-    width = own.shape[1] // 2
+        for copy in to_far + pass_on:
+            copy.wait_send()
+
+
+def correlate(white, windows, groups):
+    width = white.shape[1] // 2
     share = BAND // groups
     chunks = width // CHUNK
     fa, fd = segment_tables()
-    fd = np.stack([fd, np.zeros_like(fd)])
     vmem = pl.BlockSpec(memory_space=pltpu.VMEM)
-    block = (share, CHUNK, LAGS)
+    hbm = pl.BlockSpec(memory_space=pl.ANY)
+    block = share * CHUNK
     return pl.pallas_call(
         pair_kernel,
         out_shape=jax.ShapeDtypeStruct((share, width, LAGS), jnp.float32),
-        in_specs=[vmem] * 5,
-        out_specs=vmem,
+        in_specs=[vmem, hbm, vmem, vmem, vmem],
+        out_specs=hbm,
         scratch_shapes=[
             pltpu.VMEM((BINS, width, HELD), jnp.bfloat16),
             pltpu.VMEM((2 * BINS * BIN_PITCH, width), jnp.float32),
             pltpu.VMEM((2 * BINS * NEXT_PITCH, width), jnp.float32),
             pltpu.VMEM((OUT_ROWS * ROW_PITCH, LAGS), jnp.float32),
-            pltpu.VMEM(own.shape, jnp.bfloat16),
-            pltpu.VMEM(own.shape, jnp.bfloat16),
-            pltpu.VMEM((chunks, groups) + block, jnp.bfloat16),
-            pltpu.VMEM((chunks, 7) + block, jnp.bfloat16),
+            pltpu.VMEM((SERIES, 2 * width), jnp.bfloat16),
+            pltpu.VMEM((PAD, 2 * width), jnp.bfloat16),
+            pltpu.VMEM((PAD, width), jnp.bfloat16),
+            pltpu.VMEM((EXTRA_ROWS, width), jnp.bfloat16),
+            pltpu.VMEM((2, PAD, width), jnp.bfloat16),
+            pltpu.VMEM((chunks * groups * block, LAGS), jnp.bfloat16),
+            pltpu.VMEM((chunks * BOXES * block, LAGS), jnp.bfloat16),
+            pltpu.VMEM((2, share, CHUNK, LAGS), jnp.float32),
             pltpu.SemaphoreType.DMA((chunks, 7)),
             pltpu.SemaphoreType.DMA((chunks, 7)),
+            pltpu.SemaphoreType.DMA((PARTS + 4,)),
             pltpu.SemaphoreType.DMA((PARTS + 2,)),
-            pltpu.SemaphoreType.DMA((PARTS + 1,)),
+            pltpu.SemaphoreType.DMA((4,)),
         ],
         compiler_params=pltpu.CompilerParams(
-            vmem_limit_bytes=62 * 2**20, collective_id=0, has_side_effects=True
+            vmem_limit_bytes=63 * 2**20, collective_id=0, has_side_effects=True
         ),
-        cost_estimate=pl.CostEstimate(flops=6 * 10**9, bytes_accessed=20 * 10**6, transcendentals=0),
-    )(ya, own, jnp.asarray(fa), jnp.asarray(fd), jnp.asarray(lag_table(windows)))
-
-
-def time_series(record, starts):
-    samples = jnp.concatenate(
-        [lax.dynamic_slice_in_dim(record, starts[w], SAMP, 0) for w in range(starts.shape[0])], 1
+        cost_estimate=pl.CostEstimate(flops=6 * 10**9, bytes_accessed=24 * 10**6, transcendentals=0),
+    )(
+        white,
+        jnp.asarray(inverse_table()),
+        jnp.asarray(fa),
+        jnp.asarray(fd),
+        jnp.asarray(lag_table(windows)),
     )
-    spec = jnp.dot(jnp.asarray(dft_table()), samples, preferred_element_type=jnp.float32)
-    white = whiten(spec).reshape(2 * ROWS, samples.shape[1])
-    table = jnp.asarray(inverse_table(SEG * (SLOTS + 2)))
-    return jnp.dot(table, white, preferred_element_type=jnp.float32).astype(jnp.bfloat16)
 
 
 def body(record, starts):
     groups = lax.axis_size("tm")
-    ya = time_series(record, starts)
-    own = jnp.pad(ya[HALF : HALF + SAMP], ((0, SEG * SLOTS - SAMP), (0, 0)))
-    return correlate(ya, own, starts.shape[0] * groups, groups)
+    white = whitened(record, starts)
+    return correlate(white, starts.shape[0] * groups, groups)
 
 
 def solution(mesh):

time: 122 us -> 118 us (0.967)
  the two profiles are of different devices: /device:TPU:25 before, /device:TPU:24 now
where the time goes in v4:
time: 118 us; the launch traced here: 117 us
  Pallas kernels  115 us (97%)
  local copies, waits for them, and re-layouts  2.76 us (2%)
    pallas_call x1, Pallas kernels, correlate(): pl.pallas_call(pair_kernel, out_shape=jax.ShapeDtypeStruct((share, width,...  93.9 us
    pallas_call x1, Pallas kernels, whitened(): pl.pallas_call(white_kernel, out_shape=jax.ShapeDtypeStruct((PAD, 2 * wid...  20.8 us
    unnamed x1, local copies, waits for them, and re-layouts  2.76 us

profile of v4, /device:TPU:24, one launch (start us, length us, event | category | flops | bytes accessed | tf_op | source)
XLA Modules:
  0.0 117.4 jit_solution(1254917829695845472)
XLA Ops:
  0.0 20.8 %shard_map.73.white = bf16[3072,256]{1,0:T(8,128)(2,1)} custom-call(s32[2]{0:T(128)} %starts.1, bf16[8192,128]{1,0:T(8,128)(2,1)} %record.1, bf16[3072,3072]{1,0:T(8,128)(2,1)} %constant.10.clone.table), custom_call_target="tpu_custom_call" | custom-call | flops 5000000000 | bytes 22000000 | tf_op jit(solution)/shard_map/pallas_call | solution.py:133
  20.8 93.9 %shard_map.74 = f32[25,128,128]{2,1,0:T(8,128)} custom-call(bf16[3072,256]{1,0:T(8,128)(2,1)} %shard_map.73.white, bf16[76800,128]{1,0:T(8,128)(2,1)} %constant.11.clone.inverse, bf16[192,192]{1,0:T(8,128)(2,1)} %constant.12.clone.fa, bf16[3,192,128]{2,1,0:T(8,128)(2,1)} %constant.13.clone.fd, bf16[192,128]{1,0:T(8,128)(2,1)} %constant.14.clone.lag), custom_call_target="tpu_custom_call" | custom-call | flops 6000000000 | bytes 24000000 | tf_op jit(solution)/shard_map/pallas_call | solution.py:610
  114.7 2.8 %copy.9 = f32[25,128,128]{2,1,0:T(8,128)} copy(f32[25,128,128]{2,1,0:T(8,128)} %shard_map.74) | data formatting | bytes 3276800

commit v5 on v4

--- a/solution.py
+++ b/solution.py
@@ -12,8 +12,11 @@
 SAMP = 3000
 F = 1501
 PAD = 3072
-PIECE = 192
-PIECES = 8
+KEPT = PAD // 2
+GROUP = 384
+PIECES = 4
+BASE = 1664
+MID = 1600
 BAND = 200
 LAGS = 128
 HALF = LAGS // 2
@@ -31,26 +34,40 @@
     return 2.0 * math.pi * (np.outer(a, b) % period) / period
 
 
-def by_pieces(real, imag):
-    parts = np.zeros((2, PIECES * PIECE) + real.shape[1:], np.float32)
-    parts[0, :F], parts[1, :F] = real, imag
-    parts = parts.reshape((2, PIECES, PIECE) + real.shape[1:])
-    return np.moveaxis(parts, 0, 1).reshape((PAD,) + real.shape[1:])
+def bins_of(parity, reverse):
+    bins = 2 * np.arange(GROUP) + parity
+    bins[bins > F // 2 + 1] = -1
+    if reverse:
+        bins = np.where(bins >= 0, F - 1 - bins, -1)
+        bins[bins <= F // 2] = -1
+    else:
+        bins[bins > F // 2] = -1
+    return bins
 
 
 def dft_table():
-    angle = turns(np.arange(F), np.arange(SAMP), SAMP)
-    table = by_pieces(np.cos(angle), -np.sin(angle)) / math.sqrt(SAMP)
-    return np.pad(table, ((0, 0), (0, PAD - SAMP))).astype(BF16)
+    table = np.zeros((2, 2, GROUP, 2, KEPT), np.float32)
+    for parity in range(2):
+        bins = np.arange(parity, F // 2 + 2, 2)
+        for late in range(2):
+            angle = turns(bins, np.arange(late, SAMP, 2), SAMP)
+            table[parity, 0, : len(bins), late, : SAMP // 2] = np.cos(angle) / math.sqrt(SAMP)
+            table[parity, 1, : len(bins), late, : SAMP // 2] = -np.sin(angle) / math.sqrt(SAMP)
+    return table.reshape(KEPT, PAD).astype(BF16)
 
 
 def inverse_table():
-    time = (np.arange(SERIES) - HALF) % SAMP
-    weight = np.full((F, 1), 2.0)
-    weight[0] = weight[-1] = 1.0
-    angle = turns(np.arange(F), time, SAMP)
-    table = by_pieces(weight * np.cos(angle), -weight * np.sin(angle)).T / math.sqrt(SAMP)
-    table = table.reshape(PIECES, SERIES // PIECES, PAD // 128, 128)
+    time = (np.arange(BASE) - HALF) % SAMP
+    table = np.zeros((BASE, 2, 2, 2, GROUP), np.float32)
+    for parity in range(2):
+        for reverse in range(2):
+            bins = bins_of(parity, reverse)
+            weight = np.where(bins < 0, 0.0, np.where((bins == 0) | (bins == F - 1), 1.0, 2.0))
+            weight /= math.sqrt(SAMP)
+            angle = turns(time, np.maximum(bins, 0), SAMP)
+            table[:, parity, reverse, 0] = weight * np.cos(angle)
+            table[:, parity, reverse, 1] = -weight * np.sin(angle)
+    table = table.reshape(PIECES, BASE // PIECES, PAD // 128, 128)
     return np.moveaxis(table, 2, 1).reshape(-1, 128).astype(BF16)
 
 
@@ -81,10 +98,10 @@
 
 def white_kernel(starts, record, table, white, held, raw, wide, samples, spec, power, sems, wins):
     width = record.shape[1]
-    rows = 2 * PIECE
-    loads = []
+    loads, shifts = [], []
     for w in range(2):
         base = jnp.minimum(starts[w] // 16 * 16, record.shape[0] - TALL)
+        shifts.append(starts[w] - base)
         base = pl.multiple_of(base, 16)
         loads.append(
             pltpu.make_async_copy(record.at[pl.ds(base, TALL)], raw.at[w], wins.at[w])
@@ -92,40 +109,66 @@
         loads[w].start()
     pieces = [
         pltpu.make_async_copy(
-            table.at[pl.ds(i * rows, rows)], held.at[pl.ds(i * rows, rows)], sems.at[i]
+            table.at[pl.ds(i * GROUP, GROUP)], held.at[pl.ds(i * GROUP, GROUP)], sems.at[i]
         )
         for i in range(PIECES)
     ]
-    for piece in pieces:
-        piece.start()
-    power[:EDGE, :] = jnp.zeros((EDGE, 2 * width), jnp.float32)
-    power[EDGE + PIECES * PIECE :, :] = jnp.zeros((EDGE, 2 * width), jnp.float32)
+    pieces[0].start()
+    pieces[1].start()
+    zero = jnp.zeros((EDGE, 2 * width), jnp.float32)
+    for parity in range(2):
+        for h in range(2):
+            power[parity, h, :EDGE, :] = zero
+            power[parity, h, EDGE + GROUP :, :] = zero
     for w in range(2):
-        shift = starts[w] - jnp.minimum(starts[w] // 16 * 16, record.shape[0] - TALL)
         loads[w].wait()
         wide[w, :TALL, :] = raw[w].astype(jnp.float32)
         wide[w, TALL:, :] = jnp.zeros((wide.shape[1] - TALL, width), jnp.float32)
-        samples[:, w * width : (w + 1) * width] = wide[w, pl.ds(shift, PAD), :].astype(jnp.bfloat16)
-
-    def finish(i):
-        at = EDGE + i * PIECE
-        near = [power[at + d : at + d + PIECE, :] for d in (-1, 0, 1)]
-        smooth = (near[0] + near[1] + near[2]) / 3.0
-        factor = 1.0 / jnp.maximum(jnp.sqrt(smooth), 0.5)
+        for late in range(2):
+            samples[late, :, w * width : (w + 1) * width] = wide[
+                w, pl.ds(shifts[w] + late, KEPT, stride=2), :
+            ].astype(jnp.bfloat16)
+
+    def group(parity, h, ri):
+        first = (parity * 4 + h * 2 + ri) * GROUP
+        return slice(first, first + GROUP)
+
+    for parity in range(2):
+        squares = []
+        for ri in range(2):
+            i = parity * 2 + ri
+            pieces[i].wait()
+            part = slice(i * GROUP, (i + 1) * GROUP)
+            early, late = [
+                jnp.dot(
+                    held[part, e * KEPT : (e + 1) * KEPT], samples[e],
+                    preferred_element_type=jnp.float32,
+                )
+                for e in range(2)
+            ]
+            if i + 2 < PIECES:
+                pieces[i + 2].start()
+            both = early + late
+            turned = late - early if ri else early - late
+            spec[group(parity, 0, ri), :] = both
+            spec[group(parity, 1, ri), :] = turned
         for h in range(2):
-            part = slice(i * rows + h * PIECE, i * rows + (h + 1) * PIECE)
-            white[part, :] = (spec[part, :] * factor).astype(jnp.bfloat16)
-
-    for i in range(PIECES):
-        pieces[i].wait()
-        part = slice(i * rows, (i + 1) * rows)
-        found = jnp.dot(held[part, :], samples[...], preferred_element_type=jnp.float32)
-        spec[part, :] = found
-        real, imag = found[:PIECE], found[PIECE:]
-        power[EDGE + i * PIECE : EDGE + (i + 1) * PIECE, :] = real * real + imag * imag
-        if i:
-            finish(i - 1)
-    finish(PIECES - 1)
+            real, imag = [spec[group(parity, h, ri), :] for ri in range(2)]
+            power[parity, h, EDGE : EDGE + GROUP, :] = real * real + imag * imag
+
+    for parity in range(2):
+        for h in range(2):
+            for first in range(0, GROUP, 128):
+                at = EDGE + first
+                beside = (at, at + 1) if parity else (at - 1, at)
+                smooth = power[parity, h, at : at + 128, :]
+                for place in beside:
+                    smooth = smooth + power[1 - parity, h, place : place + 128, :]
+                factor = 1.0 / jnp.maximum(jnp.sqrt(smooth / 3.0), 0.5)
+                for ri in range(2):
+                    start = group(parity, h, ri).start + first
+                    part = slice(start, start + 128)
+                    white[part, :] = (spec[part, :] * factor).astype(jnp.bfloat16)
 
 
 def whitened(record, starts):
@@ -140,12 +183,12 @@
         ],
         out_specs=pl.BlockSpec(memory_space=pltpu.VMEM),
         scratch_shapes=[
-            pltpu.VMEM((PAD, PAD), jnp.bfloat16),
+            pltpu.VMEM((KEPT, PAD), jnp.bfloat16),
             pltpu.VMEM((2, TALL, width), jnp.bfloat16),
             pltpu.VMEM((2, PAD + 32, width), jnp.float32),
-            pltpu.VMEM((PAD, 2 * width), jnp.bfloat16),
+            pltpu.VMEM((2, KEPT, 2 * width), jnp.bfloat16),
             pltpu.VMEM((PAD, 2 * width), jnp.float32),
-            pltpu.VMEM((PIECES * PIECE + 2 * EDGE, 2 * width), jnp.float32),
+            pltpu.VMEM((2, 2, GROUP + 2 * EDGE, 2 * width), jnp.float32),
             pltpu.SemaphoreType.DMA((PIECES,)),
             pltpu.SemaphoreType.DMA((2,)),
         ],
@@ -163,6 +206,7 @@
 BOXES = 7
 RING = 4
 PARTS = 6
+WHEN = ((), (0, 3), (1, 4), (2, 5))
 BIN_PITCH = 225
 NEXT_PITCH = 129
 ROW_PITCH = 17
@@ -170,11 +214,11 @@
 EXTRA = 8
 EXTRA_ROWS = 384
 NO_FAR = 48
-KINDS = "XZXXZXZX"
+KINDS = "XZXXZZXX"
 STEPS = (
-    "b0", "b1", "s0", "b2", "f", "s1", "s2", "t0", "t1", "b3", "t2",
-    "b4", "b5", "s3", "b6", "s5", "b7", "s4", "t3", "l0", "l1", "t5",
-    "l2", "s7", "t4", "s6", "l3", "t7", "l4", "l5", "t6", "l7", "l6",
+    "b0", "b1", "b2", "s0", "f", "s2", "b3", "s1", "t0", "t2", "b4",
+    "s3", "b5", "b6", "t1", "b7", "t3", "l0", "l2", "s6", "s4", "l1",
+    "s7", "t6", "t4", "s5", "l3", "t7", "l4", "l6", "t5", "l7", "l5",
 )
 MESH = pl.DeviceIdType.MESH
 
@@ -205,7 +249,7 @@
     def behind(distance):
         return {"chan": lax.rem(j + blocks + distance, blocks)}
 
-    piece = SERIES // PIECES
+    piece = BASE // PIECES
     area = piece * (PAD // 128)
     tables = [
         pltpu.make_async_copy(
@@ -252,24 +296,37 @@
     ]
 
     lane = lax.broadcasted_iota(jnp.int32, (SEG, width), 1)
-    begun = 0
+    done = MID
     for c in range(PIECES):
         tables[c].wait()
-        total = jnp.zeros((piece, 2 * width), jnp.float32)
-        for p in range(0, PAD // 128, 2):
-            first = c % 2 * area + p * piece
-            block = jnp.concatenate(
-                [part[first : first + piece, :], part[first + piece : first + 2 * piece, :]], 1
-            )
-            total += jnp.dot(
-                block, white[p * 128 : (p + 2) * 128, :], preferred_element_type=jnp.float32
-            )
-        ya[c * piece : (c + 1) * piece, :] = total.astype(jnp.bfloat16)
+        halves = []
+        for parity in range(2):
+            total = jnp.zeros((piece, 2 * width), jnp.float32)
+            for p in range(parity * KEPT // 128, (parity + 1) * KEPT // 128, 2):
+                first = c % 2 * area + p * piece
+                block = jnp.concatenate(
+                    [part[first : first + piece, :], part[first + piece : first + 2 * piece, :]], 1
+                )
+                total += jnp.dot(
+                    block, white[p * 128 : (p + 2) * 128, :], preferred_element_type=jnp.float32
+                )
+            halves.append(total)
         if c + 2 < PIECES:
             tables[c + 2].start()
-        while begun < PARTS and SEG + (begun + 1) * length <= (c + 1) * piece:
-            to_near[begun].start()
-            begun += 1
+        first, end = c * piece, (c + 1) * piece
+        kept = min(end, MID) - first
+        ya[first : first + kept, :] = (halves[0] + halves[1])[:kept].astype(jnp.bfloat16)
+        later = halves[0] - halves[1]
+        for w in range(2):
+            rows[w * BASE + first : w * BASE + end, :] = later[:, w * width : (w + 1) * width]
+        ready = (end + SAMP // 2) // 16 * 16
+        for w in range(2):
+            source = slice(w * BASE + done - SAMP // 2, w * BASE + ready - SAMP // 2)
+            ya[done:ready, w * width : (w + 1) * width] = rows[source, :].astype(jnp.bfloat16)
+        done = ready
+        for p in WHEN[c]:
+            to_near[p].start()
+    ya[done:, :] = jnp.zeros((SERIES - done, 2 * width), jnp.bfloat16)
 
     def pack_segments(index):
         for s in index:
@@ -417,13 +474,20 @@
     unrolled(BINS, gram_own, 8)
     unrolled(SLOTS, pack_segments, 8)
     unrolled(EXTRA_ROWS // SEG, pack_extra, 1)
-    for p in range(PARTS):
+    for p in sum(WHEN, ()):
         to_near[p].wait_recv()
+        if p == WHEN[-1][0]:
+
+            @pl.when(odd)
+            def _():
+                for copy in to_far:
+                    copy.start()
+
         short_segments(near_block, 1, j == blocks - 1, p * (SLOTS // PARTS), SLOTS // PARTS)
 
     @pl.when(odd)
     def _():
-        for copy in to_far + pass_on:
+        for copy in pass_on:
             copy.start()
 
     unrolled(BINS, gram_next, 8)

time: 118 us -> 97.1 us (0.82)
  the two profiles are of different devices: /device:TPU:24 before, /device:TPU:25 now
where the time goes in v5:
time: 97.1 us; the launch traced here: 96.9 us
  Pallas kernels  94.1 us (97%)
  local copies, waits for them, and re-layouts  2.76 us (3%)
    pallas_call x1, Pallas kernels, correlate(): pl.pallas_call(pair_kernel, out_shape=jax.ShapeDtypeStruct((share, width,...  84.2 us
    pallas_call x1, Pallas kernels, whitened(): pl.pallas_call(white_kernel, out_shape=jax.ShapeDtypeStruct((PAD, 2 * wid...  9.89 us
    unnamed x1, local copies, waits for them, and re-layouts  2.76 us

profile of v5, /device:TPU:25, one launch (start us, length us, event | category | flops | bytes accessed | tf_op | source)
XLA Modules:
  0.0 96.9 jit_solution(18420671265706466170)
XLA Ops:
  0.0 9.9 %shard_map.73.white = bf16[3072,256]{1,0:T(8,128)(2,1)} custom-call(s32[2]{0:T(128)} %starts.1, bf16[8192,128]{1,0:T(8,128)(2,1)} %record.1, bf16[1536,3072]{1,0:T(8,128)(2,1)} %constant.10.clone.table), custom_call_target="tpu_custom_call" | custom-call | flops 5000000000 | bytes 22000000 | tf_op jit(solution)/shard_map/pallas_call | solution.py:176
  9.9 84.2 %shard_map.74 = f32[25,128,128]{2,1,0:T(8,128)} custom-call(bf16[3072,256]{1,0:T(8,128)(2,1)} %shard_map.73.white, bf16[39936,128]{1,0:T(8,128)(2,1)} %constant.11.clone.inverse, bf16[192,192]{1,0:T(8,128)(2,1)} %constant.12.clone.fa, bf16[3,192,128]{2,1,0:T(8,128)(2,1)} %constant.13.clone.fd, bf16[192,128]{1,0:T(8,128)(2,1)} %constant.14.clone.lag), custom_call_target="tpu_custom_call" | custom-call | flops 6000000000 | bytes 24000000 | tf_op jit(solution)/shard_map/pallas_call | solution.py:674
  94.1 2.8 %copy.9 = f32[25,128,128]{2,1,0:T(8,128)} copy(f32[25,128,128]{2,1,0:T(8,128)} %shard_map.74) | data formatting | bytes 3276800

commit v6 on v5

--- a/solution.py
+++ b/solution.py
@@ -1,3 +1,4 @@
+import functools
 import math
 
 import jax
@@ -109,12 +110,12 @@
         loads[w].start()
     pieces = [
         pltpu.make_async_copy(
-            table.at[pl.ds(i * GROUP, GROUP)], held.at[pl.ds(i * GROUP, GROUP)], sems.at[i]
-        )
-        for i in range(PIECES)
+            table.at[pl.ds(i * 2 * GROUP, 2 * GROUP)], held.at[pl.ds(i * 2 * GROUP, 2 * GROUP)],
+            sems.at[i],
+        )
+        for i in range(2)
     ]
     pieces[0].start()
-    pieces[1].start()
     zero = jnp.zeros((EDGE, 2 * width), jnp.float32)
     for parity in range(2):
         for h in range(2):
@@ -134,24 +135,21 @@
         return slice(first, first + GROUP)
 
     for parity in range(2):
-        squares = []
+        pieces[parity].wait()
+        if parity == 0:
+            pieces[1].start()
+        part = slice(parity * 2 * GROUP, (parity + 1) * 2 * GROUP)
+        early, late = [
+            jnp.dot(
+                held[part, e * KEPT : (e + 1) * KEPT], samples[e],
+                preferred_element_type=jnp.float32,
+            )
+            for e in range(2)
+        ]
         for ri in range(2):
-            i = parity * 2 + ri
-            pieces[i].wait()
-            part = slice(i * GROUP, (i + 1) * GROUP)
-            early, late = [
-                jnp.dot(
-                    held[part, e * KEPT : (e + 1) * KEPT], samples[e],
-                    preferred_element_type=jnp.float32,
-                )
-                for e in range(2)
-            ]
-            if i + 2 < PIECES:
-                pieces[i + 2].start()
-            both = early + late
-            turned = late - early if ri else early - late
-            spec[group(parity, 0, ri), :] = both
-            spec[group(parity, 1, ri), :] = turned
+            one, two = [found[ri * GROUP : (ri + 1) * GROUP] for found in (early, late)]
+            spec[group(parity, 0, ri), :] = one + two
+            spec[group(parity, 1, ri), :] = two - one if ri else one - two
         for h in range(2):
             real, imag = [spec[group(parity, h, ri), :] for ri in range(2)]
             power[parity, h, EDGE : EDGE + GROUP, :] = real * real + imag * imag
@@ -205,8 +203,6 @@
 CHUNK = 16
 BOXES = 7
 RING = 4
-PARTS = 6
-WHEN = ((), (0, 3), (1, 4), (2, 5))
 BIN_PITCH = 225
 NEXT_PITCH = 129
 ROW_PITCH = 17
@@ -272,30 +268,196 @@
             device_id=device, device_id_type=MESH,
         )
 
-    length = SLOTS // PARTS * SEG
+    spans, turns_long, turns_short = [], [], []
+    done, began, fresh = MID, (0, MID // SEG), (0, MID // SEG - 1)
+    for c in range(PIECES):
+        first, end = c * piece, (c + 1) * piece
+        ready = (end + SAMP // 2) // 16 * 16
+        low_end = min(end, MID)
+        spans.append(((max(first, SEG), low_end), (done, min(ready, SEG * (SLOTS + 1)))))
+        done = ready
+        final = c == PIECES - 1
+        stop = (
+            MID // SEG if final else (end - SPAN) // SEG + 1,
+            SLOTS if final else (ready - SPAN) // SEG + 1,
+        )
+        turns_long.append([s for h in range(2) for s in range(began[h], stop[h])])
+        began = stop
+        stop = (
+            MID // SEG - 1 if final else end // SEG - 1,
+            SLOTS if final else ready // SEG - 1,
+        )
+        turns_short.append([s for h in range(2) for s in range(fresh[h], stop[h])])
+        fresh = stop
+    parts = 2 * PIECES
     to_near = [
         remote(
-            ya.at[pl.ds(SEG + p * length, length)], near.at[pl.ds(p * length, length)],
-            sent_y.at[p], come_y.at[p], behind(-1),
-        )
-        for p in range(PARTS)
+            ya.at[pl.ds(first, end - first)], near.at[pl.ds(first - SEG, end - first)],
+            sent_y.at[2 * c + h], come_y.at[2 * c + h], behind(-1),
+        )
+        for c in range(PIECES)
+        for h, (first, end) in enumerate(spans[c])
     ]
     to_far = [
-        remote(pack, far.at[0], sent_y.at[PARTS], come_y.at[PARTS], behind(-2)),
+        remote(pack, far.at[0], sent_y.at[parts], come_y.at[parts], behind(-2)),
         remote(
             extra, far.at[1, pl.ds(0, EXTRA_ROWS)],
-            sent_y.at[PARTS + 1], come_y.at[PARTS + 1], behind(-2),
+            sent_y.at[parts + 1], come_y.at[parts + 1], behind(-2),
         ),
     ]
     pass_on = [
         remote(
             near.at[:, pl.ds(w * width, width)], far.at[w],
-            sent_y.at[PARTS + 2 + w], come_y.at[PARTS + w], behind(-1),
+            sent_y.at[parts + 2 + w], come_y.at[parts + w], behind(-1),
         )
         for w in range(2)
     ]
 
     lane = lax.broadcasted_iota(jnp.int32, (SEG, width), 1)
+    def pack_segments(index):
+        for s in index:
+            block = ya[pl.ds(pl.multiple_of((s + 1) * SEG, SEG), SEG), :].astype(jnp.float32)
+            turned = pltpu.roll(block[:, width:], width // 2, 1)
+            pack[pl.ds(pl.multiple_of(s * SEG, SEG), SEG), :] = jnp.where(
+                lane < width // 2, block[:, :width], turned
+            ).astype(jnp.bfloat16)
+
+    def pack_extra(index):
+        for e in index:
+            total = jnp.zeros((SEG, width), jnp.float32)
+            for g in range(PAD // EXTRA_ROWS):
+                first = pl.multiple_of((e + 1) * SEG, SEG) + g * EXTRA_ROWS
+                block = ya[pl.ds(first, SEG), :].astype(jnp.float32)
+                for w in range(2):
+                    place = (2 * g + w) * EXTRA
+                    turned = pltpu.roll(
+                        block[:, w * width : (w + 1) * width], (place + width // 2) % width, 1
+                    )
+                    total = jnp.where((lane >= place) & (lane < place + EXTRA), turned, total)
+            extra[pl.ds(pl.multiple_of(e * SEG, SEG), SEG), :] = total.astype(jnp.bfloat16)
+
+    def far_block(s):
+        group, row = s // (EXTRA_ROWS // SEG), lax.rem(s, EXTRA_ROWS // SEG)
+        first = far[0, pl.ds(pl.multiple_of(s * SEG, SEG), SEG), :].astype(jnp.float32)
+        row = jnp.where(odd, row, s)
+        rest = far[1, pl.ds(pl.multiple_of(row * SEG, SEG), SEG), :].astype(jnp.float32)
+        half = width // 2
+        both = []
+        for w in range(2):
+            body = first if w == 0 else pltpu.roll(first, half, 1)
+            turn = lax.rem(half + width - (2 * group + w) * EXTRA, width)
+            both.append(jnp.where(lane < half, body, pltpu.roll(rest, turn, 1)))
+        block = jnp.concatenate(
+            [jnp.where(odd, both[0], first), jnp.where(odd, both[1], rest)], 1
+        )
+        return block.astype(jnp.bfloat16)
+
+    def spread(slot, s, spec):
+        at = slot * SECOND + s
+        bins[pl.ds(at, 2 * BINS, stride=BIN_PITCH), :] = spec[:, :width]
+        bins[pl.ds(at + SLOTS, 2 * BINS, stride=BIN_PITCH), :] = spec[:, width:]
+
+    def long_segments(index):
+        specs = []
+        for s in index:
+            block = ya[s * SEG : s * SEG + SPAN, :]
+            specs.append(jnp.dot(fa[...], block, preferred_element_type=jnp.float32))
+        for s, spec in zip(index, specs):
+            spread(1, s, spec)
+
+    def short_batch(block_of, slot, absent, index):
+        specs = []
+        for s in index:
+            block = block_of(s)
+            twice = jnp.concatenate([block, block], 0)
+            if isinstance(s, int):
+                kind = 0 if s < FULL else 2 if s == FULL else 1
+            else:
+                kind = jnp.where(s < FULL, 0, jnp.where(s == FULL, 2, 1))
+            if absent is not None:
+                kind = jnp.where(absent, 1, kind)
+            specs.append(jnp.dot(fd[kind], twice, preferred_element_type=jnp.float32))
+        for s, spec in zip(index, specs):
+            spread(slot, s, spec)
+
+    def short_segments(block_of, slot, absent):
+        unrolled(SLOTS, functools.partial(short_batch, block_of, slot, absent), 8)
+
+    def place_of(s):
+        return s * SEG if isinstance(s, int) else pl.multiple_of(s * SEG, SEG)
+
+    def own_block(s):
+        return ya[pl.ds(place_of(s + 1), SEG), :]
+
+    def near_block(s):
+        return near[pl.ds(place_of(s), SEG), :]
+
+    def of_bin(slot, b):
+        first = b * 2 * BIN_PITCH + slot * SECOND
+        return bins[pl.ds(first, 2 * SLOTS), :], bins[pl.ds(first + BIN_PITCH, 2 * SLOTS), :]
+
+    def product(slot, b, first):
+        real, imag = [part.astype(jnp.bfloat16) for part in of_bin(slot, b)]
+        both = jnp.concatenate(
+            [jnp.concatenate([real, imag], 0), jnp.concatenate([-imag, real], 0)], 1
+        )
+        return jnp.dot(sega[b, first:, :], both, preferred_element_type=jnp.float32)
+
+    def keep(target, pitch, b, cross):
+        first = b * 2 * pitch
+        target[pl.ds(first, width), :] = cross[:, :width]
+        target[pl.ds(first + pitch, width), :] = cross[:, width:]
+
+    def gram_next(index):
+        for b, cross in zip(index, [product(1, b, 0) for b in index]):
+            keep(gram, NEXT_PITCH, b, cross)
+
+    def gram_own(index):
+        for b in index:
+            sega[b] = jnp.concatenate(of_bin(1, b), 0).astype(jnp.bfloat16).T
+        for b, cross in zip(index, [product(0, b, 0) for b in index]):
+            keep(bins, BIN_PITCH, b, cross)
+
+    tall = width - NO_FAR
+    same = lax.broadcasted_iota(jnp.int32, (tall, width), 1)
+    same = same > lax.broadcasted_iota(jnp.int32, (tall, width), 0) + NO_FAR
+
+    def gram_far(index):
+        crosses = [product(1, b, NO_FAR) for b in index]
+        places = [pl.ds((2 * b + h) * BIN_PITCH + NO_FAR, tall) for b in index for h in range(2)]
+        before = [bins[place, :] for place in places]
+        for e, place in enumerate(places):
+            h = e % 2
+            cross = crosses[e // 2][:, h * width : (h + 1) * width]
+            bins[place, :] = jnp.where(same, before[e], cross)
+
+    def place_next(ahead, c):
+        return width + ahead - c
+
+    def place_own(ahead, c):
+        return jnp.where(ahead + 7 > c, ahead - c, 2 * width + ahead - c)
+
+    def lag_step(source, pitch, place, base):
+        def step(index):
+            cross = jnp.concatenate(
+                [
+                    source[pl.ds(base + c, 2 * BINS, stride=pitch), :].astype(jnp.bfloat16)
+                    for c in index
+                ],
+                1,
+            )
+            lags = lax.dot_general(
+                cross, lag[...], (((0,), (0,)), ((), ())), preferred_element_type=jnp.float32
+            )
+            for u, c in enumerate(index):
+                for e in range(width // 8):
+                    k = jnp.clip(place(8 * e, base + c), -FIRST, BAND + 1)
+                    at = u * width + 8 * e
+                    first = (k + FIRST) * ROW_PITCH + c
+                    rows[pl.ds(first, 8, stride=ROW_PITCH), :] = lags[at : at + 8]
+
+        return step
+
     done = MID
     for c in range(PIECES):
         tables[c].wait()
@@ -324,166 +486,31 @@
             source = slice(w * BASE + done - SAMP // 2, w * BASE + ready - SAMP // 2)
             ya[done:ready, w * width : (w + 1) * width] = rows[source, :].astype(jnp.bfloat16)
         done = ready
-        for p in WHEN[c]:
-            to_near[p].start()
-    ya[done:, :] = jnp.zeros((SERIES - done, 2 * width), jnp.bfloat16)
-
-    def pack_segments(index):
-        for s in index:
-            block = ya[pl.ds(pl.multiple_of((s + 1) * SEG, SEG), SEG), :].astype(jnp.float32)
-            turned = pltpu.roll(block[:, width:], width // 2, 1)
-            pack[pl.ds(pl.multiple_of(s * SEG, SEG), SEG), :] = jnp.where(
-                lane < width // 2, block[:, :width], turned
-            ).astype(jnp.bfloat16)
-
-    def pack_extra(index):
-        for e in index:
-            total = jnp.zeros((SEG, width), jnp.float32)
-            for g in range(PAD // EXTRA_ROWS):
-                first = pl.multiple_of((e + 1) * SEG, SEG) + g * EXTRA_ROWS
-                block = ya[pl.ds(first, SEG), :].astype(jnp.float32)
-                for w in range(2):
-                    place = (2 * g + w) * EXTRA
-                    turned = pltpu.roll(
-                        block[:, w * width : (w + 1) * width], (place + width // 2) % width, 1
-                    )
-                    total = jnp.where((lane >= place) & (lane < place + EXTRA), turned, total)
-            extra[pl.ds(pl.multiple_of(e * SEG, SEG), SEG), :] = total.astype(jnp.bfloat16)
-
-    def far_block(s):
-        group, row = s // (EXTRA_ROWS // SEG), lax.rem(s, EXTRA_ROWS // SEG)
-        first = far[0, pl.ds(pl.multiple_of(s * SEG, SEG), SEG), :].astype(jnp.float32)
-        row = jnp.where(odd, row, s)
-        rest = far[1, pl.ds(pl.multiple_of(row * SEG, SEG), SEG), :].astype(jnp.float32)
-        half = width // 2
-        both = []
-        for w in range(2):
-            body = first if w == 0 else pltpu.roll(first, half, 1)
-            turn = lax.rem(half + width - (2 * group + w) * EXTRA, width)
-            both.append(jnp.where(lane < half, body, pltpu.roll(rest, turn, 1)))
-        block = jnp.concatenate(
-            [jnp.where(odd, both[0], first), jnp.where(odd, both[1], rest)], 1
-        )
-        return block.astype(jnp.bfloat16)
-
-    def spread(slot, s, spec):
-        at = slot * SECOND + s
-        bins[pl.ds(at, 2 * BINS, stride=BIN_PITCH), :] = spec[:, :width]
-        bins[pl.ds(at + SLOTS, 2 * BINS, stride=BIN_PITCH), :] = spec[:, width:]
-
-    def long_segments(index):
-        specs = []
-        for s in index:
-            block = ya[pl.ds(pl.multiple_of(s * SEG, SEG), SPAN), :]
-            specs.append(jnp.dot(fa[...], block, preferred_element_type=jnp.float32))
-        for s, spec in zip(index, specs):
-            spread(0, s, spec)
-
-    def short_segments(block_of, slot, absent, first, count):
-        def step(index):
-            specs = []
-            for s in index:
-                s = first + s
-                block = block_of(s)
-                twice = jnp.concatenate([block, block], 0)
-                kind = jnp.where(s < FULL, 0, jnp.where(s == FULL, 2, 1))
-                kind = jnp.where(absent, 1, kind)
-                specs.append(jnp.dot(fd[kind], twice, preferred_element_type=jnp.float32))
-            for s, spec in zip(index, specs):
-                spread(slot, first + s, spec)
-
-        unrolled(count, step, 8)
-
-    def own_block(s):
-        return ya[pl.ds(pl.multiple_of((s + 1) * SEG, SEG), SEG), :]
-
-    def near_block(s):
-        return near[pl.ds(pl.multiple_of(s * SEG, SEG), SEG), :]
-
-    def of_bin(slot, b):
-        first = b * 2 * BIN_PITCH + slot * SECOND
-        return bins[pl.ds(first, 2 * SLOTS), :], bins[pl.ds(first + BIN_PITCH, 2 * SLOTS), :]
-
-    def turn_bins(index):
-        for b in index:
-            sega[b] = jnp.concatenate(of_bin(0, b), 0).astype(jnp.bfloat16).T
-
-    def product(slot, b, first):
-        real, imag = [part.astype(jnp.bfloat16) for part in of_bin(slot, b)]
-        both = jnp.concatenate(
-            [jnp.concatenate([real, imag], 0), jnp.concatenate([-imag, real], 0)], 1
-        )
-        return jnp.dot(sega[b, first:, :], both, preferred_element_type=jnp.float32)
-
-    def keep(target, pitch, b, cross):
-        first = b * 2 * pitch
-        target[pl.ds(first, width), :] = cross[:, :width]
-        target[pl.ds(first + pitch, width), :] = cross[:, width:]
-
-    def gram_next(index):
-        for b, cross in zip(index, [product(1, b, 0) for b in index]):
-            keep(gram, NEXT_PITCH, b, cross)
-
-    def gram_own(index):
-        for b, cross in zip(index, [product(0, b, 0) for b in index]):
-            keep(bins, BIN_PITCH, b, cross)
-
-    tall = width - NO_FAR
-    same = lax.broadcasted_iota(jnp.int32, (tall, width), 1)
-    same = same > lax.broadcasted_iota(jnp.int32, (tall, width), 0) + NO_FAR
-
-    def gram_far(index):
-        crosses = [product(1, b, NO_FAR) for b in index]
-        places = [pl.ds((2 * b + h) * BIN_PITCH + NO_FAR, tall) for b in index for h in range(2)]
-        before = [bins[place, :] for place in places]
-        for e, place in enumerate(places):
-            h = e % 2
-            cross = crosses[e // 2][:, h * width : (h + 1) * width]
-            bins[place, :] = jnp.where(same, before[e], cross)
-
-    def place_next(ahead, c):
-        return width + ahead - c
-
-    def place_own(ahead, c):
-        return jnp.where(ahead + 7 > c, ahead - c, 2 * width + ahead - c)
-
-    def lag_step(source, pitch, place, base):
-        def step(index):
-            cross = jnp.concatenate(
-                [
-                    source[pl.ds(base + c, 2 * BINS, stride=pitch), :].astype(jnp.bfloat16)
-                    for c in index
-                ],
-                1,
-            )
-            lags = lax.dot_general(
-                cross, lag[...], (((0,), (0,)), ((), ())), preferred_element_type=jnp.float32
-            )
-            for u, c in enumerate(index):
-                for e in range(width // 8):
-                    k = jnp.clip(place(8 * e, base + c), -FIRST, BAND + 1)
-                    at = u * width + 8 * e
-                    first = (k + FIRST) * ROW_PITCH + c
-                    rows[pl.ds(first, 8, stride=ROW_PITCH), :] = lags[at : at + 8]
-
-        return step
-
-    unrolled(SLOTS, long_segments, 8)
-    unrolled(BINS, turn_bins, 8)
-    short_segments(own_block, 0, False, 0, SLOTS)
+        if c == PIECES - 1:
+            ya[done:, :] = jnp.zeros((SERIES - done, 2 * width), jnp.bfloat16)
+        for h in range(2):
+            to_near[2 * c + h].start()
+        long_segments(turns_long[c])
+        short_batch(own_block, 0, None, turns_short[c])
+
     unrolled(BINS, gram_own, 8)
-    unrolled(SLOTS, pack_segments, 8)
-    unrolled(EXTRA_ROWS // SEG, pack_extra, 1)
-    for p in sum(WHEN, ()):
-        to_near[p].wait_recv()
-        if p == WHEN[-1][0]:
+
+    @pl.when(odd)
+    def _():
+        unrolled(SLOTS, pack_segments, 16)
+        unrolled(EXTRA_ROWS // SEG, pack_extra, 6)
+
+    for c in range(PIECES):
+        for h in range(2):
+            to_near[2 * c + h].wait_recv()
+        if c == PIECES - 1:
 
             @pl.when(odd)
             def _():
                 for copy in to_far:
                     copy.start()
 
-        short_segments(near_block, 1, j == blocks - 1, p * (SLOTS // PARTS), SLOTS // PARTS)
+        short_batch(near_block, 1, j == blocks - 1, turns_short[c])
 
     @pl.when(odd)
     def _():
@@ -503,7 +530,7 @@
             for copy in pass_on:
                 copy.wait_recv()
 
-        short_segments(far_block, 1, j >= blocks - 2, 0, SLOTS)
+        short_segments(far_block, 1, j >= blocks - 2)
         unrolled(BINS, gram_far, 8)
 
     def at(column, row):
@@ -691,8 +718,8 @@
             pltpu.VMEM((2, share, CHUNK, LAGS), jnp.float32),
             pltpu.SemaphoreType.DMA((chunks, 7)),
             pltpu.SemaphoreType.DMA((chunks, 7)),
-            pltpu.SemaphoreType.DMA((PARTS + 4,)),
-            pltpu.SemaphoreType.DMA((PARTS + 2,)),
+            pltpu.SemaphoreType.DMA((2 * PIECES + 4,)),
+            pltpu.SemaphoreType.DMA((2 * PIECES + 2,)),
             pltpu.SemaphoreType.DMA((4,)),
         ],
         compiler_params=pltpu.CompilerParams(

time: 97.1 us -> 95.4 us (0.982)
  Pallas kernels: 94.1 us -> 91.7 us
    pallas_call x1, Pallas kernels: 84.2 us -> 82.1 us  [correlate(): pl.pallas_call(pair_kernel, out_shape=jax.ShapeDtypeStruct((share, width,...]
where the time goes in v6:
time: 95.4 us; the launch traced here: 94.5 us
  Pallas kernels  91.7 us (96%)
  local copies, waits for them, and re-layouts  2.76 us (3%)
    pallas_call x1, Pallas kernels, correlate(): pl.pallas_call(pair_kernel, out_shape=jax.ShapeDtypeStruct((share, width,...  82.1 us
    pallas_call x1, Pallas kernels, whitened(): pl.pallas_call(white_kernel, out_shape=jax.ShapeDtypeStruct((PAD, 2 * wid...  9.61 us
    unnamed x1, local copies, waits for them, and re-layouts  2.76 us

profile of v6, /device:TPU:25, one launch (start us, length us, event | category | flops | bytes accessed | tf_op | source)
XLA Modules:
  0.0 94.5 jit_solution(4752332223248441969)
XLA Ops:
  0.0 9.6 %shard_map.73.white = bf16[3072,256]{1,0:T(8,128)(2,1)} custom-call(s32[2]{0:T(128)} %starts.1, bf16[8192,128]{1,0:T(8,128)(2,1)} %record.1, bf16[1536,3072]{1,0:T(8,128)(2,1)} %constant.10.clone.table), custom_call_target="tpu_custom_call" | custom-call | flops 5000000000 | bytes 22000000 | tf_op jit(solution)/shard_map/pallas_call | solution.py:174
  9.6 82.1 %shard_map.74 = f32[25,128,128]{2,1,0:T(8,128)} custom-call(bf16[3072,256]{1,0:T(8,128)(2,1)} %shard_map.73.white, bf16[39936,128]{1,0:T(8,128)(2,1)} %constant.11.clone.inverse, bf16[192,192]{1,0:T(8,128)(2,1)} %constant.12.clone.fa, bf16[3,192,128]{2,1,0:T(8,128)(2,1)} %constant.13.clone.fd, bf16[192,128]{1,0:T(8,128)(2,1)} %constant.14.clone.lag), custom_call_target="tpu_custom_call" | custom-call | flops 6000000000 | bytes 24000000 | tf_op jit(solution)/shard_map/pallas_call | solution.py:701
  91.7 2.8 %copy.9 = f32[25,128,128]{2,1,0:T(8,128)} copy(f32[25,128,128]{2,1,0:T(8,128)} %shard_map.74) | data formatting | bytes 3276800

commit v7 on v6

--- a/solution.py
+++ b/solution.py
@@ -210,11 +210,11 @@
 EXTRA = 8
 EXTRA_ROWS = 384
 NO_FAR = 48
-KINDS = "XZXXZZXX"
+KINDS = "XXZXZXXZ"
 STEPS = (
-    "b0", "b1", "b2", "s0", "f", "s2", "b3", "s1", "t0", "t2", "b4",
-    "s3", "b5", "b6", "t1", "b7", "t3", "l0", "l2", "s6", "s4", "l1",
-    "s7", "t6", "t4", "s5", "l3", "t7", "l4", "l6", "t5", "l7", "l5",
+    "b0", "b1", "b2", "s0", "f", "t0", "s1", "s2", "b3", "b4", "t1",
+    "t2", "b5", "b6", "s3", "b7", "l0", "l2", "s5", "s4", "l1", "s6",
+    "t3", "t5", "s7", "t4", "l3", "t6", "l5", "t7", "l4", "l6", "l7",
 )
 MESH = pl.DeviceIdType.MESH
 
@@ -274,7 +274,7 @@
         first, end = c * piece, (c + 1) * piece
         ready = (end + SAMP // 2) // 16 * 16
         low_end = min(end, MID)
-        spans.append(((max(first, SEG), low_end), (done, min(ready, SEG * (SLOTS + 1)))))
+        spans.append(((max(first, SEG), low_end), (done, min(ready, SEG * SLOTS))))
         done = ready
         final = c == PIECES - 1
         stop = (
@@ -312,6 +312,17 @@
         )
         for w in range(2)
     ]
+
+    has_near, has_far = j < blocks - 1, j < blocks - 2
+    near[SEG * (SLOTS - 1) :, :] = jnp.zeros((SEG, 2 * width), jnp.bfloat16)
+
+    @pl.when(jnp.logical_not(has_near))
+    def _():
+        near[: SEG * (SLOTS - 1), :] = jnp.zeros((SEG * (SLOTS - 1), 2 * width), jnp.bfloat16)
+
+    @pl.when(jnp.logical_not(has_far))
+    def _():
+        far[...] = jnp.zeros(far.shape, jnp.bfloat16)
 
     lane = lax.broadcasted_iota(jnp.int32, (SEG, width), 1)
     def pack_segments(index):
@@ -488,8 +499,12 @@
         done = ready
         if c == PIECES - 1:
             ya[done:, :] = jnp.zeros((SERIES - done, 2 * width), jnp.bfloat16)
-        for h in range(2):
-            to_near[2 * c + h].start()
+
+        @pl.when(j > 0)
+        def _():
+            for h in range(2):
+                to_near[2 * c + h].start()
+
         long_segments(turns_long[c])
         short_batch(own_block, 0, None, turns_short[c])
 
@@ -501,18 +516,22 @@
         unrolled(EXTRA_ROWS // SEG, pack_extra, 6)
 
     for c in range(PIECES):
-        for h in range(2):
-            to_near[2 * c + h].wait_recv()
+
+        @pl.when(has_near)
+        def _():
+            for h in range(2):
+                to_near[2 * c + h].wait_recv()
+
         if c == PIECES - 1:
 
-            @pl.when(odd)
+            @pl.when(odd & (j > 1))
             def _():
                 for copy in to_far:
                     copy.start()
 
         short_batch(near_block, 1, j == blocks - 1, turns_short[c])
 
-    @pl.when(odd)
+    @pl.when(odd & has_near)
     def _():
         for copy in pass_on:
             copy.start()
@@ -520,12 +539,12 @@
     unrolled(BINS, gram_next, 8)
 
     def take_far():
-        @pl.when(odd)
+        @pl.when(odd & has_far)
         def _():
             for copy in to_far:
                 copy.wait_recv()
 
-        @pl.when(jnp.logical_not(odd))
+        @pl.when(jnp.logical_not(odd) & has_far)
         def _():
             for copy in pass_on:
                 copy.wait_recv()
@@ -681,12 +700,20 @@
 
     for n in ending.values():
         result(n).wait()
-    for copy in to_near:
-        copy.wait_send()
-
-    @pl.when(odd)
+
+    @pl.when(j > 0)
     def _():
-        for copy in to_far + pass_on:
+        for copy in to_near:
+            copy.wait_send()
+
+    @pl.when(odd & (j > 1))
+    def _():
+        for copy in to_far:
+            copy.wait_send()
+
+    @pl.when(odd & has_near)
+    def _():
+        for copy in pass_on:
             copy.wait_send()
 
 

time: 95.4 us -> 94.6 us (level)
  the two profiles are of different devices: /device:TPU:25 before, /device:TPU:120 now
where the time goes in v7:
time: 94.6 us; the launch traced here: 94.4 us
  Pallas kernels  91.6 us (97%)
  local copies, waits for them, and re-layouts  2.76 us (3%)
    pallas_call x1, Pallas kernels, correlate(): pl.pallas_call(pair_kernel, out_shape=jax.ShapeDtypeStruct((share, width,...  82 us
    pallas_call x1, Pallas kernels, whitened(): pl.pallas_call(white_kernel, out_shape=jax.ShapeDtypeStruct((PAD, 2 * wid...  9.61 us
    unnamed x1, local copies, waits for them, and re-layouts  2.76 us

profile of v7, /device:TPU:120, one launch (start us, length us, event | category | flops | bytes accessed | tf_op | source)
XLA Modules:
  0.0 94.4 jit_solution(4964817865172455976)
XLA Ops:
  0.0 9.6 %shard_map.73.white = bf16[3072,256]{1,0:T(8,128)(2,1)} custom-call(s32[2]{0:T(128)} %starts.1, bf16[8192,128]{1,0:T(8,128)(2,1)} %record.1, bf16[1536,3072]{1,0:T(8,128)(2,1)} %constant.10.clone.table), custom_call_target="tpu_custom_call" | custom-call | flops 5000000000 | bytes 22000000 | tf_op jit(solution)/shard_map/pallas_call | solution.py:174
  9.6 82.0 %shard_map.74 = f32[25,128,128]{2,1,0:T(8,128)} custom-call(bf16[3072,256]{1,0:T(8,128)(2,1)} %shard_map.73.white, bf16[39936,128]{1,0:T(8,128)(2,1)} %constant.11.clone.inverse, bf16[192,192]{1,0:T(8,128)(2,1)} %constant.12.clone.fa, bf16[3,192,128]{2,1,0:T(8,128)(2,1)} %constant.13.clone.fd, bf16[192,128]{1,0:T(8,128)(2,1)} %constant.14.clone.lag), custom_call_target="tpu_custom_call" | custom-call | flops 6000000000 | bytes 24000000 | tf_op jit(solution)/shard_map/pallas_call | solution.py:728
  91.6 2.8 %copy.9 = f32[25,128,128]{2,1,0:T(8,128)} copy(f32[25,128,128]{2,1,0:T(8,128)} %shard_map.74) | data formatting | bytes 3276800

commit v8 on v7

--- a/solution.py
+++ b/solution.py
@@ -260,7 +260,6 @@
     peers = (right, left, other, behind(-1), behind(1), behind(-2), behind(2))
     for device in peers:
         pl.semaphore_signal(barrier, inc=1, device_id=device, device_id_type=MESH)
-    pl.semaphore_wait(barrier, len(peers))
 
     def remote(source, target, send, receive, device):
         return pltpu.make_async_remote_copy(
@@ -499,6 +498,8 @@
         done = ready
         if c == PIECES - 1:
             ya[done:, :] = jnp.zeros((SERIES - done, 2 * width), jnp.bfloat16)
+        if c == 0:
+            pl.semaphore_wait(barrier, len(peers))
 
         @pl.when(j > 0)
         def _():

time: 94.6 us -> 94.6 us (level)
  no operation moved by 1% of the time
where the time goes in v8:
time: 94.6 us; the launch traced here: 94.4 us
  Pallas kernels  91.6 us (97%)
  local copies, waits for them, and re-layouts  2.76 us (3%)
    pallas_call x1, Pallas kernels, correlate(): pl.pallas_call(pair_kernel, out_shape=jax.ShapeDtypeStruct((share, width,...  82 us
    pallas_call x1, Pallas kernels, whitened(): pl.pallas_call(white_kernel, out_shape=jax.ShapeDtypeStruct((PAD, 2 * wid...  9.61 us
    unnamed x1, local copies, waits for them, and re-layouts  2.76 us

profile of v8, /device:TPU:120, one launch (start us, length us, event | category | flops | bytes accessed | tf_op | source)
XLA Modules:
  0.0 94.4 jit_solution(8310693915574993666)
XLA Ops:
  0.0 9.6 %shard_map.73.white = bf16[3072,256]{1,0:T(8,128)(2,1)} custom-call(s32[2]{0:T(128)} %starts.1, bf16[8192,128]{1,0:T(8,128)(2,1)} %record.1, bf16[1536,3072]{1,0:T(8,128)(2,1)} %constant.10.clone.table), custom_call_target="tpu_custom_call" | custom-call | flops 5000000000 | bytes 22000000 | tf_op jit(solution)/shard_map/pallas_call | solution.py:174
  9.6 82.0 %shard_map.74 = f32[25,128,128]{2,1,0:T(8,128)} custom-call(bf16[3072,256]{1,0:T(8,128)(2,1)} %shard_map.73.white, bf16[39936,128]{1,0:T(8,128)(2,1)} %constant.11.clone.inverse, bf16[192,192]{1,0:T(8,128)(2,1)} %constant.12.clone.fa, bf16[3,192,128]{2,1,0:T(8,128)(2,1)} %constant.13.clone.fd, bf16[192,128]{1,0:T(8,128)(2,1)} %constant.14.clone.lag), custom_call_target="tpu_custom_call" | custom-call | flops 6000000000 | bytes 24000000 | tf_op jit(solution)/shard_map/pallas_call | solution.py:729
  91.6 2.8 %copy.9 = f32[25,128,128]{2,1,0:T(8,128)} copy(f32[25,128,128]{2,1,0:T(8,128)} %shard_map.74) | data formatting | bytes 3276800
